TPU v7x, 128 devices: a whole 4x4x4 slice. The times are simulated.
128 devices in a mesh: gx: 16 (over z, y), yz: 8 (over x, core).
Axes of the slice: x: 4, y: 4, z: 4, core: 2. Of those that a mesh axis runs over, the one named last changes fastest.
Arguments:
- positions: float32 [3, 8192, 256], P(None, ('gx', 'yz')), may hold values from -3 to 3
- velocity: float32 [3, 8192, 256], P(None, ('gx', 'yz')), may hold values from -6 to 6
- energy: float32 [8192, 256], P(('gx', 'yz')), may hold values from 0.5 to 2
- masses: float32 [8192, 256], P(('gx', 'yz')), may hold values from 0.002 to 0.008
- smoothing_bins: int32 [8192, 256], P(('gx', 'yz')), may hold values from 0 to 5
- counts: int32 [8192], P(('gx', 'yz')), may hold values from 8 to 256, as said below
- exports: int32 [4096], P(('gx', 'yz')), may hold values from 0 to 63, as said below
- cross_pairs: int32 [2, 32768], P(None, ('gx', 'yz')), may hold values from 0 to 287, as said below
- local_pairs: int32 [2, 8192], P(None, ('gx', 'yz')), may hold values from 0 to 63, as said below
Outputs:
- density: float32 [8192, 256], P(('gx', 'yz'))
- acceleration: float32 [3, 8192, 256], P(None, ('gx', 'yz'))
- energy_rate: float32 [8192, 256], P(('gx', 'yz'))
Inputs may be any that keep to these rules, and one draw needn't show every extreme that they name: `counts`: each device has some cell holding exactly 256 live particles; the mean count differs from device to device. `exports`: each device's block of 32 entries lists distinct local cells. `cross_pairs`: row 0 is a local cell of the device that holds the column; row 1 is an import slot (3 a + b) * 32 + k with (a, b) never (1, 1). A device's block of 256 columns holds 32 columns for each of the directions (a, b) = (1, 2), (2, 0), (2, 1), (2, 2), then for (1, 0), (0, 2), (0, 1), (0, 0). Each column of the first half is mirrored by exactly one column of the second half on the device that owns its imported cell, naming the same two cells, and no two columns of a block name the same two cells. `local_pairs`: both rows hold local cells of the device that holds the column; they differ in every column.
All inputs are finite; a program needn't handle non-finite values.
Results may differ from a plain program's by a relative error of at most 0.0003.
Values sent between devices are 32-bit elements; how exact they have to be, the bound alone decides.
A program may use at most 64 MiB of HBM per device.

v0:
```python
import jax
import jax.numpy as jnp
from jax import lax
from jax.sharding import PartitionSpec as P

SIGMA_NORM = 0.3183098861837907
GAMMA_GAS = 5.0 / 3.0
ALPHA_VISC = 1.0
BETA_VISC = 2.0


def shifted(block, axis, distance):
    devices = range(lax.axis_size(axis))
    route = [((i - distance) % len(devices), i) for i in devices]
    return lax.ppermute(block, axis, route)


def with_halo(cells, sides, width):
    for axis, dim in sides:
        count = lax.axis_size(axis)
        head = lax.slice_in_dim(cells, 0, width, axis=dim)
        tail = lax.slice_in_dim(cells, cells.shape[dim] - width, cells.shape[dim], axis=dim)
        cells = jnp.concatenate(
            [
                lax.ppermute(tail, axis, [(i, (i + 1) % count) for i in range(count)]),
                cells,
                lax.ppermute(head, axis, [((i + 1) % count, i) for i in range(count)]),
            ],
            axis=dim,
        )
    return cells


def spline_value(scaled):
    inner_part = 1.0 - 1.5 * scaled**2 + 0.75 * scaled**3
    outer_part = 0.25 * jnp.maximum(2.0 - scaled, 0.0) ** 3
    return jnp.where(scaled < 1.0, inner_part, outer_part)


def spline_slope(scaled):
    inner_part = -3.0 + 2.25 * scaled
    outer_part = -0.75 * jnp.maximum(2.0 - scaled, 0.0) ** 2 / jnp.maximum(scaled, 1.0)
    return jnp.where(scaled < 1.0, inner_part, outer_part)


def separation(target, source):
    diff_x = target[:, 0, :, None] - source[:, 0, None, :]
    diff_y = target[:, 1, :, None] - source[:, 1, None, :]
    diff_z = target[:, 2, :, None] - source[:, 2, None, :]
    return (diff_x, diff_y, diff_z)


def density_block(target, source):
    diff_x, diff_y, diff_z = separation(target, source)
    radius = jnp.sqrt(diff_x * diff_x + diff_y * diff_y + diff_z * diff_z)
    smooth = target[:, 3, :, None]
    weight = spline_value(radius / smooth) * (SIGMA_NORM / smooth**3)
    return jnp.sum(weight * source[:, 4, None, :], axis=2)


def force_block(target, source):
    diff_x, diff_y, diff_z = separation(target, source)
    dist_sq = diff_x * diff_x + diff_y * diff_y + diff_z * diff_z
    radius = jnp.sqrt(dist_sq)
    smooth_target = target[:, 3, :, None]
    smooth_source = source[:, 3, None, :]
    grad_mean = 0.5 * (
        spline_slope(radius / smooth_target) * (SIGMA_NORM / smooth_target**5)
        + spline_slope(radius / smooth_source) * (SIGMA_NORM / smooth_source**5)
    )
    vel_x = target[:, 5, :, None] - source[:, 5, None, :]
    vel_y = target[:, 6, :, None] - source[:, 6, None, :]
    vel_z = target[:, 7, :, None] - source[:, 7, None, :]
    approach = vel_x * diff_x + vel_y * diff_y + vel_z * diff_z
    smooth_mean = 0.5 * (smooth_target + smooth_source)
    converge = smooth_mean * jnp.minimum(approach, 0.0) / (dist_sq + 0.01 * smooth_mean**2)
    sound_mean = 0.5 * (target[:, 10, :, None] + source[:, 10, None, :])
    density_mean = 0.5 * (target[:, 8, :, None] + source[:, 8, None, :])
    viscous = (BETA_VISC * converge**2 - ALPHA_VISC * sound_mean * converge) / density_mean
    press_target = target[:, 9, :, None]
    press_source = source[:, 9, None, :]
    common = (press_target + press_source + viscous) * grad_mean
    mass_target = target[:, 4, :, None]
    mass_source = source[:, 4, None, :]
    pull_target = mass_source * common
    pull_source = mass_target * common
    work_rate = grad_mean * approach
    target_part = jnp.stack(
        [
            -jnp.sum(pull_target * diff_x, axis=2),
            -jnp.sum(pull_target * diff_y, axis=2),
            -jnp.sum(pull_target * diff_z, axis=2),
            jnp.sum(mass_source * (press_target + 0.5 * viscous) * work_rate, axis=2),
        ],
        axis=1,
    )
    source_part = jnp.stack(
        [
            jnp.sum(pull_source * diff_x, axis=1),
            jnp.sum(pull_source * diff_y, axis=1),
            jnp.sum(pull_source * diff_z, axis=1),
            jnp.sum(mass_target * (press_source + 0.5 * viscous) * work_rate, axis=1),
        ],
        axis=1,
    )
    return (target_part, source_part)


def density_pass(cell_data, source_table, targets, sources):
    cell_count = cell_data.shape[0]
    slot_count = cell_data.shape[2]
    block_count = targets.shape[0] // 16
    cell_range = jnp.arange(cell_count, dtype=jnp.int32)

    def density_accumulate(running, id_pair):
        target_ids, source_ids = id_pair
        contribution = density_block(cell_data[target_ids], source_table[source_ids])
        select = (cell_range[:, None] == target_ids[None, :]).astype(jnp.float32)
        added = jnp.dot(
            select,
            contribution,
            precision=lax.Precision.HIGHEST,
            preferred_element_type=jnp.float32,
        )
        return (running + added, None)

    running, unused = lax.scan(
        density_accumulate,
        jnp.zeros((cell_count, slot_count), jnp.float32),
        (targets.reshape(block_count, 16), sources.reshape(block_count, 16)),
    )
    return running


def force_pass(cell_data, source_table, targets, sources, return_slots, slot_total):
    cell_count = cell_data.shape[0]
    slot_count = cell_data.shape[2]
    block_count = targets.shape[0] // 16
    cell_range = jnp.arange(cell_count, dtype=jnp.int32)
    slot_range = jnp.arange(slot_total, dtype=jnp.int32)

    def force_accumulate(carried, id_triple):
        own_sum, returned = carried
        target_ids, source_ids, slot_ids = id_triple
        target_part, source_part = force_block(cell_data[target_ids], source_table[source_ids])
        select = (cell_range[:, None] == target_ids[None, :]).astype(jnp.float32)
        select_slot = (slot_range[:, None] == slot_ids[None, :]).astype(jnp.float32)
        own_sum = own_sum + jnp.dot(
            select,
            target_part.reshape(16, 4 * slot_count),
            precision=lax.Precision.HIGHEST,
            preferred_element_type=jnp.float32,
        )
        returned = returned + jnp.dot(
            select_slot,
            source_part.reshape(16, 4 * slot_count),
            precision=lax.Precision.HIGHEST,
            preferred_element_type=jnp.float32,
        )
        return ((own_sum, returned), None)

    start = (
        jnp.zeros((cell_count, 4 * slot_count), jnp.float32),
        jnp.zeros((slot_total, 4 * slot_count), jnp.float32),
    )
    carried, unused = lax.scan(
        force_accumulate,
        start,
        (
            targets.reshape(block_count, 16),
            sources.reshape(block_count, 16),
            return_slots.reshape(block_count, 16),
        ),
    )
    return carried


def send_back_gx(partial_value):
    return shifted(partial_value, "gx", 1)


def send_back_yz(partial_value, step_by):
    return shifted(partial_value, "yz", step_by)


def body(
    positions, velocity, energy, masses, smoothing_bins, counts, exports, cross_pairs, local_pairs
):
    cell_count = positions.shape[1]
    slot_count = positions.shape[2]
    export_count = exports.shape[0]
    live_mask = (
        lax.broadcasted_iota(jnp.int32, (cell_count, slot_count), 1) < counts[:, None]
    ).astype(jnp.float32)
    smooth = 0.4 * 1.2 ** smoothing_bins.astype(jnp.float32)
    particle_mass = masses * live_mask
    base = jnp.concatenate(
        [jnp.transpose(positions, (1, 0, 2)), smooth[:, None], particle_mass[:, None]], axis=1
    )
    outgoing = base[exports]
    received = with_halo(outgoing[None, None], (("gx", 0), ("yz", 1)), 1)
    imported = received.reshape(9 * export_count, 5, slot_count)
    source_table = jnp.concatenate([base, imported], axis=0)
    cell_range = jnp.arange(cell_count, dtype=jnp.int32)
    targets = jnp.concatenate([cell_range, local_pairs[0], cross_pairs[0]])
    sources = jnp.concatenate([cell_range, local_pairs[1], cross_pairs[1] + cell_count])
    raw_density = density_pass(base, source_table, targets, sources)
    rho = jnp.where(live_mask > 0, raw_density, 1.0)
    pressure_term = (GAMMA_GAS - 1.0) * energy / rho
    sound_speed = jnp.sqrt(GAMMA_GAS * (GAMMA_GAS - 1.0) * energy)
    new_fields = jnp.stack(
        [velocity[0], velocity[1], velocity[2], rho, pressure_term, sound_speed], axis=1
    )
    forcing = jnp.concatenate([base, new_fields], axis=1)
    payload = forcing[exports]
    upward = shifted(payload, "gx", -1)
    sideways = []
    for operand, step_by in ((upward[None], 1), (jnp.stack([upward, payload]), -1)):
        sideways.append(shifted(operand, "yz", step_by))
    lower_side = sideways[0][0]
    upper_corner = sideways[1][0]
    beside_upper = sideways[1][1]
    empty_blocks = jnp.zeros((5 * export_count, payload.shape[1], slot_count), jnp.float32)
    used_blocks = jnp.concatenate(
        [empty_blocks, beside_upper, lower_side, upward, upper_corner], axis=0
    )
    force_table = jnp.concatenate([forcing, used_blocks], axis=0)
    upper_count = cross_pairs.shape[1] // 2
    upper_pairs = cross_pairs[:, :upper_count]
    force_targets = jnp.concatenate([cell_range, local_pairs[0], upper_pairs[0]])
    force_sources = jnp.concatenate([cell_range, local_pairs[1], upper_pairs[1] + cell_count])
    return_slots = jnp.concatenate(
        [-jnp.ones((cell_count + local_pairs.shape[1],), jnp.int32), upper_pairs[1]]
    )
    own_sum, returned = force_pass(
        forcing, force_table, force_targets, force_sources, return_slots, 9 * export_count
    )
    blocks = returned.reshape(3, 3, export_count, 4 * slot_count)
    middle = blocks[1] + send_back_gx(blocks[2])
    folded = middle[1]
    for column, step_by in ((0, -1), (2, 1)):
        folded = folded + send_back_yz(middle[column], step_by)
    export_select = (cell_range[:, None] == exports[None, :]).astype(jnp.float32)
    own_sum = own_sum + jnp.dot(
        export_select, folded, precision=lax.Precision.HIGHEST, preferred_element_type=jnp.float32
    )
    totals = own_sum.reshape(cell_count, 4, slot_count)
    acceleration = jnp.transpose(totals[:, :3], (1, 0, 2)) * live_mask[None]
    energy_rate = totals[:, 3] * live_mask
    return (raw_density * live_mask, acceleration, energy_rate)


def solution(mesh):
    return jax.shard_map(
        body,
        mesh=mesh,
        in_specs=(
            P(None, ("gx", "yz"), None),
            P(None, ("gx", "yz"), None),
            P(("gx", "yz"), None),
            P(("gx", "yz"), None),
            P(("gx", "yz"), None),
            P(("gx", "yz")),
            P(("gx", "yz")),
            P(None, ("gx", "yz")),
            P(None, ("gx", "yz")),
        ),
        out_specs=(P(("gx", "yz"), None), P(None, ("gx", "yz"), None), P(("gx", "yz"), None)),
        check_vma=False,
    )
```

profile of v0, /device:TPU:1, one launch (start us, length us, event | category | flops | bytes accessed | tf_op | source)
XLA Modules:
  0.0 1236.6 jit_solution(10377616990764529724)
XLA Ops:
  31.5 389.0 %while.24 = (s32[]{:T(128)}, f32[64,256]{1,0:T(8,128)}, s32[24,16]{1,0:T(8,128)}, f32[64,5,256]{2,1,0:T(8,128)S(1)}, s32[24,16]{1,0:T(8,128)}, /*index=5*/f32[352,5,256]{2,1,0:T(8,128)S(1)}, s32[]{:T(128)}, s32[]{:T(128)}) while((s32[]{:T(128)}, f32[64,256]{1,0:T(8,128)}, s32[24,16]{1,0:T(8,128)}, f32[64,5,256]{2,1,0:T(8,128)S(1)}, ...), condition=%wide.region_2.3_spmd.clone, body=%wide.region_0.2_spmd.clone.sunk | while | flops 29404256 | bytes 1205031 | solution.py:127
  457.8 758.3 %while.25 = (s32[]{:T(128)}, f32[64,1024]{1,0:T(8,128)S(1)}, f32[288,1024]{1,0:T(8,128)S(1)}, s32[16,16]{1,0:T(8,128)S(1)}, s32[16,16]{1,0:T(8,128)S(1)}, /*inde...) while((s32[]{:T(128)}, f32[64,1024]{1,0:T(8,128)S(1)}, ...), condition=%wide.region_12.13_spmd.clone, body=%wide.region_3.12_spmd.clone.sunk | while | flops 286051936 | bytes 7103480 | solution.py:166
  474.7 15.9 %fusion.90 = (f32[16,256]{1,0:T(8,128)S(1)}, f32[16,256]{1,0:T(8,128)S(1)}, f32[16,256]{1,0:T(8,128)S(1)}, f32[16,256]{1,0:T(8,128)S(1)}, f32[16,256]{1,0:T(8,128)S(1)}, /*index=5*/f32[16,256]{1,0:T(8,128)S(1)}) fusion(f32[16,256]{1,0:T(8,128)S(1)} %bitcast.376, f32[16,256]{1,0:T(8,128)S(1)} %bitcast.339, f32[16,256]{1,0:T(8,128)S(1)} %bitcast.342, ...), kind=kLoop, calls=%fused_computation.66.clone.1 | loop fusion | flops 79667200 | bytes 491520 | tf_op jit(solution)/shard_map/while/body/eval_jaxpr/reduce_sum | solution.py:101
  491.4 13.4 %multiply_reduce_fusion.4 = f32[16,256]{1,0:T(8,128)S(1)} fusion(f32[16,256]{1,0:T(8,128)S(1)} %bitcast.369, f32[16,256]{1,0:T(8,128)S(1)} %bitcast.371, f32[16,256]{1,0:T(8,128)S(1)} %bitcast.322, f32[16,256]{1,0:T(8,128)S(1)} %bitcast.325, f32[16,256]{1,0:T(8,128)S(1)} %bitcast.328, f32[16,256]{1,0:T(8,128)S(1)} %bitcast.331, ...), kind=kLoop, calls=%fused_computation.68.clone.1 | loop fusion | flops 68153344 | bytes 376832 | tf_op jit(solution)/shard_map/while/body/eval_jaxpr/reduce_sum | solution.py:93
  522.0 15.9 %fusion.90 = (f32[16,256]{1,0:T(8,128)S(1)}, f32[16,256]{1,0:T(8,128)S(1)}, f32[16,256]{1,0:T(8,128)S(1)}, f32[16,256]{1,0:T(8,128)S(1)}, f32[16,256]{1,0:T(8,128)S(1)}, /*index=5*/f32[16,256]{1,0:T(8,128)S(1)}) fusion(f32[16,256]{1,0:T(8,128)S(1)} %bitcast.376, f32[16,256]{1,0:T(8,128)S(1)} %bitcast.339, f32[16,256]{1,0:T(8,128)S(1)} %bitcast.342, ...), kind=kLoop, calls=%fused_computation.66.clone.1 | loop fusion | flops 79667200 | bytes 491520 | tf_op jit(solution)/shard_map/while/body/eval_jaxpr/reduce_sum | solution.py:101
  538.8 13.4 %multiply_reduce_fusion.4 = f32[16,256]{1,0:T(8,128)S(1)} fusion(f32[16,256]{1,0:T(8,128)S(1)} %bitcast.369, f32[16,256]{1,0:T(8,128)S(1)} %bitcast.371, f32[16,256]{1,0:T(8,128)S(1)} %bitcast.322, f32[16,256]{1,0:T(8,128)S(1)} %bitcast.325, f32[16,256]{1,0:T(8,128)S(1)} %bitcast.328, f32[16,256]{1,0:T(8,128)S(1)} %bitcast.331, ...), kind=kLoop, calls=%fused_computation.68.clone.1 | loop fusion | flops 68153344 | bytes 376832 | tf_op jit(solution)/shard_map/while/body/eval_jaxpr/reduce_sum | solution.py:93
  569.4 15.9 %fusion.90 = (f32[16,256]{1,0:T(8,128)S(1)}, f32[16,256]{1,0:T(8,128)S(1)}, f32[16,256]{1,0:T(8,128)S(1)}, f32[16,256]{1,0:T(8,128)S(1)}, f32[16,256]{1,0:T(8,128)S(1)}, /*index=5*/f32[16,256]{1,0:T(8,128)S(1)}) fusion(f32[16,256]{1,0:T(8,128)S(1)} %bitcast.376, f32[16,256]{1,0:T(8,128)S(1)} %bitcast.339, f32[16,256]{1,0:T(8,128)S(1)} %bitcast.342, ...), kind=kLoop, calls=%fused_computation.66.clone.1 | loop fusion | flops 79667200 | bytes 491520 | tf_op jit(solution)/shard_map/while/body/eval_jaxpr/reduce_sum | solution.py:101
  586.2 13.4 %multiply_reduce_fusion.4 = f32[16,256]{1,0:T(8,128)S(1)} fusion(f32[16,256]{1,0:T(8,128)S(1)} %bitcast.369, f32[16,256]{1,0:T(8,128)S(1)} %bitcast.371, f32[16,256]{1,0:T(8,128)S(1)} %bitcast.322, f32[16,256]{1,0:T(8,128)S(1)} %bitcast.325, f32[16,256]{1,0:T(8,128)S(1)} %bitcast.328, f32[16,256]{1,0:T(8,128)S(1)} %bitcast.331, ...), kind=kLoop, calls=%fused_computation.68.clone.1 | loop fusion | flops 68153344 | bytes 376832 | tf_op jit(solution)/shard_map/while/body/eval_jaxpr/reduce_sum | solution.py:93
  616.8 15.9 %fusion.90 = (f32[16,256]{1,0:T(8,128)S(1)}, f32[16,256]{1,0:T(8,128)S(1)}, f32[16,256]{1,0:T(8,128)S(1)}, f32[16,256]{1,0:T(8,128)S(1)}, f32[16,256]{1,0:T(8,128)S(1)}, /*index=5*/f32[16,256]{1,0:T(8,128)S(1)}) fusion(f32[16,256]{1,0:T(8,128)S(1)} %bitcast.376, f32[16,256]{1,0:T(8,128)S(1)} %bitcast.339, f32[16,256]{1,0:T(8,128)S(1)} %bitcast.342, ...), kind=kLoop, calls=%fused_computation.66.clone.1 | loop fusion | flops 79667200 | bytes 491520 | tf_op jit(solution)/shard_map/while/body/eval_jaxpr/reduce_sum | solution.py:101
  633.6 13.4 %multiply_reduce_fusion.4 = f32[16,256]{1,0:T(8,128)S(1)} fusion(f32[16,256]{1,0:T(8,128)S(1)} %bitcast.369, f32[16,256]{1,0:T(8,128)S(1)} %bitcast.371, f32[16,256]{1,0:T(8,128)S(1)} %bitcast.322, f32[16,256]{1,0:T(8,128)S(1)} %bitcast.325, f32[16,256]{1,0:T(8,128)S(1)} %bitcast.328, f32[16,256]{1,0:T(8,128)S(1)} %bitcast.331, ...), kind=kLoop, calls=%fused_computation.68.clone.1 | loop fusion | flops 68153344 | bytes 376832 | tf_op jit(solution)/shard_map/while/body/eval_jaxpr/reduce_sum | solution.py:93
  664.2 15.9 %fusion.90 = (f32[16,256]{1,0:T(8,128)S(1)}, f32[16,256]{1,0:T(8,128)S(1)}, f32[16,256]{1,0:T(8,128)S(1)}, f32[16,256]{1,0:T(8,128)S(1)}, f32[16,256]{1,0:T(8,128)S(1)}, /*index=5*/f32[16,256]{1,0:T(8,128)S(1)}) fusion(f32[16,256]{1,0:T(8,128)S(1)} %bitcast.376, f32[16,256]{1,0:T(8,128)S(1)} %bitcast.339, f32[16,256]{1,0:T(8,128)S(1)} %bitcast.342, ...), kind=kLoop, calls=%fused_computation.66.clone.1 | loop fusion | flops 79667200 | bytes 491520 | tf_op jit(solution)/shard_map/while/body/eval_jaxpr/reduce_sum | solution.py:101
  681.0 13.4 %multiply_reduce_fusion.4 = f32[16,256]{1,0:T(8,128)S(1)} fusion(f32[16,256]{1,0:T(8,128)S(1)} %bitcast.369, f32[16,256]{1,0:T(8,128)S(1)} %bitcast.371, f32[16,256]{1,0:T(8,128)S(1)} %bitcast.322, f32[16,256]{1,0:T(8,128)S(1)} %bitcast.325, f32[16,256]{1,0:T(8,128)S(1)} %bitcast.328, f32[16,256]{1,0:T(8,128)S(1)} %bitcast.331, ...), kind=kLoop, calls=%fused_computation.68.clone.1 | loop fusion | flops 68153344 | bytes 376832 | tf_op jit(solution)/shard_map/while/body/eval_jaxpr/reduce_sum | solution.py:93
  711.6 15.9 %fusion.90 = (f32[16,256]{1,0:T(8,128)S(1)}, f32[16,256]{1,0:T(8,128)S(1)}, f32[16,256]{1,0:T(8,128)S(1)}, f32[16,256]{1,0:T(8,128)S(1)}, f32[16,256]{1,0:T(8,128)S(1)}, /*index=5*/f32[16,256]{1,0:T(8,128)S(1)}) fusion(f32[16,256]{1,0:T(8,128)S(1)} %bitcast.376, f32[16,256]{1,0:T(8,128)S(1)} %bitcast.339, f32[16,256]{1,0:T(8,128)S(1)} %bitcast.342, ...), kind=kLoop, calls=%fused_computation.66.clone.1 | loop fusion | flops 79667200 | bytes 491520 | tf_op jit(solution)/shard_map/while/body/eval_jaxpr/reduce_sum | solution.py:101
  728.4 13.4 %multiply_reduce_fusion.4 = f32[16,256]{1,0:T(8,128)S(1)} fusion(f32[16,256]{1,0:T(8,128)S(1)} %bitcast.369, f32[16,256]{1,0:T(8,128)S(1)} %bitcast.371, f32[16,256]{1,0:T(8,128)S(1)} %bitcast.322, f32[16,256]{1,0:T(8,128)S(1)} %bitcast.325, f32[16,256]{1,0:T(8,128)S(1)} %bitcast.328, f32[16,256]{1,0:T(8,128)S(1)} %bitcast.331, ...), kind=kLoop, calls=%fused_computation.68.clone.1 | loop fusion | flops 68153344 | bytes 376832 | tf_op jit(solution)/shard_map/while/body/eval_jaxpr/reduce_sum | solution.py:93
  759.0 15.9 %fusion.90 = (f32[16,256]{1,0:T(8,128)S(1)}, f32[16,256]{1,0:T(8,128)S(1)}, f32[16,256]{1,0:T(8,128)S(1)}, f32[16,256]{1,0:T(8,128)S(1)}, f32[16,256]{1,0:T(8,128)S(1)}, /*index=5*/f32[16,256]{1,0:T(8,128)S(1)}) fusion(f32[16,256]{1,0:T(8,128)S(1)} %bitcast.376, f32[16,256]{1,0:T(8,128)S(1)} %bitcast.339, f32[16,256]{1,0:T(8,128)S(1)} %bitcast.342, ...), kind=kLoop, calls=%fused_computation.66.clone.1 | loop fusion | flops 79667200 | bytes 491520 | tf_op jit(solution)/shard_map/while/body/eval_jaxpr/reduce_sum | solution.py:101
  775.8 13.4 %multiply_reduce_fusion.4 = f32[16,256]{1,0:T(8,128)S(1)} fusion(f32[16,256]{1,0:T(8,128)S(1)} %bitcast.369, f32[16,256]{1,0:T(8,128)S(1)} %bitcast.371, f32[16,256]{1,0:T(8,128)S(1)} %bitcast.322, f32[16,256]{1,0:T(8,128)S(1)} %bitcast.325, f32[16,256]{1,0:T(8,128)S(1)} %bitcast.328, f32[16,256]{1,0:T(8,128)S(1)} %bitcast.331, ...), kind=kLoop, calls=%fused_computation.68.clone.1 | loop fusion | flops 68153344 | bytes 376832 | tf_op jit(solution)/shard_map/while/body/eval_jaxpr/reduce_sum | solution.py:93
  806.4 15.9 %fusion.90 = (f32[16,256]{1,0:T(8,128)S(1)}, f32[16,256]{1,0:T(8,128)S(1)}, f32[16,256]{1,0:T(8,128)S(1)}, f32[16,256]{1,0:T(8,128)S(1)}, f32[16,256]{1,0:T(8,128)S(1)}, /*index=5*/f32[16,256]{1,0:T(8,128)S(1)}) fusion(f32[16,256]{1,0:T(8,128)S(1)} %bitcast.376, f32[16,256]{1,0:T(8,128)S(1)} %bitcast.339, f32[16,256]{1,0:T(8,128)S(1)} %bitcast.342, ...), kind=kLoop, calls=%fused_computation.66.clone.1 | loop fusion | flops 79667200 | bytes 491520 | tf_op jit(solution)/shard_map/while/body/eval_jaxpr/reduce_sum | solution.py:101
  823.2 13.4 %multiply_reduce_fusion.4 = f32[16,256]{1,0:T(8,128)S(1)} fusion(f32[16,256]{1,0:T(8,128)S(1)} %bitcast.369, f32[16,256]{1,0:T(8,128)S(1)} %bitcast.371, f32[16,256]{1,0:T(8,128)S(1)} %bitcast.322, f32[16,256]{1,0:T(8,128)S(1)} %bitcast.325, f32[16,256]{1,0:T(8,128)S(1)} %bitcast.328, f32[16,256]{1,0:T(8,128)S(1)} %bitcast.331, ...), kind=kLoop, calls=%fused_computation.68.clone.1 | loop fusion | flops 68153344 | bytes 376832 | tf_op jit(solution)/shard_map/while/body/eval_jaxpr/reduce_sum | solution.py:93
  853.8 15.9 %fusion.90 = (f32[16,256]{1,0:T(8,128)S(1)}, f32[16,256]{1,0:T(8,128)S(1)}, f32[16,256]{1,0:T(8,128)S(1)}, f32[16,256]{1,0:T(8,128)S(1)}, f32[16,256]{1,0:T(8,128)S(1)}, /*index=5*/f32[16,256]{1,0:T(8,128)S(1)}) fusion(f32[16,256]{1,0:T(8,128)S(1)} %bitcast.376, f32[16,256]{1,0:T(8,128)S(1)} %bitcast.339, f32[16,256]{1,0:T(8,128)S(1)} %bitcast.342, ...), kind=kLoop, calls=%fused_computation.66.clone.1 | loop fusion | flops 79667200 | bytes 491520 | tf_op jit(solution)/shard_map/while/body/eval_jaxpr/reduce_sum | solution.py:101
  870.6 13.4 %multiply_reduce_fusion.4 = f32[16,256]{1,0:T(8,128)S(1)} fusion(f32[16,256]{1,0:T(8,128)S(1)} %bitcast.369, f32[16,256]{1,0:T(8,128)S(1)} %bitcast.371, f32[16,256]{1,0:T(8,128)S(1)} %bitcast.322, f32[16,256]{1,0:T(8,128)S(1)} %bitcast.325, f32[16,256]{1,0:T(8,128)S(1)} %bitcast.328, f32[16,256]{1,0:T(8,128)S(1)} %bitcast.331, ...), kind=kLoop, calls=%fused_computation.68.clone.1 | loop fusion | flops 68153344 | bytes 376832 | tf_op jit(solution)/shard_map/while/body/eval_jaxpr/reduce_sum | solution.py:93
  901.2 15.9 %fusion.90 = (f32[16,256]{1,0:T(8,128)S(1)}, f32[16,256]{1,0:T(8,128)S(1)}, f32[16,256]{1,0:T(8,128)S(1)}, f32[16,256]{1,0:T(8,128)S(1)}, f32[16,256]{1,0:T(8,128)S(1)}, /*index=5*/f32[16,256]{1,0:T(8,128)S(1)}) fusion(f32[16,256]{1,0:T(8,128)S(1)} %bitcast.376, f32[16,256]{1,0:T(8,128)S(1)} %bitcast.339, f32[16,256]{1,0:T(8,128)S(1)} %bitcast.342, ...), kind=kLoop, calls=%fused_computation.66.clone.1 | loop fusion | flops 79667200 | bytes 491520 | tf_op jit(solution)/shard_map/while/body/eval_jaxpr/reduce_sum | solution.py:101
  918.0 13.4 %multiply_reduce_fusion.4 = f32[16,256]{1,0:T(8,128)S(1)} fusion(f32[16,256]{1,0:T(8,128)S(1)} %bitcast.369, f32[16,256]{1,0:T(8,128)S(1)} %bitcast.371, f32[16,256]{1,0:T(8,128)S(1)} %bitcast.322, f32[16,256]{1,0:T(8,128)S(1)} %bitcast.325, f32[16,256]{1,0:T(8,128)S(1)} %bitcast.328, f32[16,256]{1,0:T(8,128)S(1)} %bitcast.331, ...), kind=kLoop, calls=%fused_computation.68.clone.1 | loop fusion | flops 68153344 | bytes 376832 | tf_op jit(solution)/shard_map/while/body/eval_jaxpr/reduce_sum | solution.py:93
  948.6 15.9 %fusion.90 = (f32[16,256]{1,0:T(8,128)S(1)}, f32[16,256]{1,0:T(8,128)S(1)}, f32[16,256]{1,0:T(8,128)S(1)}, f32[16,256]{1,0:T(8,128)S(1)}, f32[16,256]{1,0:T(8,128)S(1)}, /*index=5*/f32[16,256]{1,0:T(8,128)S(1)}) fusion(f32[16,256]{1,0:T(8,128)S(1)} %bitcast.376, f32[16,256]{1,0:T(8,128)S(1)} %bitcast.339, f32[16,256]{1,0:T(8,128)S(1)} %bitcast.342, ...), kind=kLoop, calls=%fused_computation.66.clone.1 | loop fusion | flops 79667200 | bytes 491520 | tf_op jit(solution)/shard_map/while/body/eval_jaxpr/reduce_sum | solution.py:101
  965.4 13.4 %multiply_reduce_fusion.4 = f32[16,256]{1,0:T(8,128)S(1)} fusion(f32[16,256]{1,0:T(8,128)S(1)} %bitcast.369, f32[16,256]{1,0:T(8,128)S(1)} %bitcast.371, f32[16,256]{1,0:T(8,128)S(1)} %bitcast.322, f32[16,256]{1,0:T(8,128)S(1)} %bitcast.325, f32[16,256]{1,0:T(8,128)S(1)} %bitcast.328, f32[16,256]{1,0:T(8,128)S(1)} %bitcast.331, ...), kind=kLoop, calls=%fused_computation.68.clone.1 | loop fusion | flops 68153344 | bytes 376832 | tf_op jit(solution)/shard_map/while/body/eval_jaxpr/reduce_sum | solution.py:93
  996.0 15.9 %fusion.90 = (f32[16,256]{1,0:T(8,128)S(1)}, f32[16,256]{1,0:T(8,128)S(1)}, f32[16,256]{1,0:T(8,128)S(1)}, f32[16,256]{1,0:T(8,128)S(1)}, f32[16,256]{1,0:T(8,128)S(1)}, /*index=5*/f32[16,256]{1,0:T(8,128)S(1)}) fusion(f32[16,256]{1,0:T(8,128)S(1)} %bitcast.376, f32[16,256]{1,0:T(8,128)S(1)} %bitcast.339, f32[16,256]{1,0:T(8,128)S(1)} %bitcast.342, ...), kind=kLoop, calls=%fused_computation.66.clone.1 | loop fusion | flops 79667200 | bytes 491520 | tf_op jit(solution)/shard_map/while/body/eval_jaxpr/reduce_sum | solution.py:101
  1012.8 13.4 %multiply_reduce_fusion.4 = f32[16,256]{1,0:T(8,128)S(1)} fusion(f32[16,256]{1,0:T(8,128)S(1)} %bitcast.369, f32[16,256]{1,0:T(8,128)S(1)} %bitcast.371, f32[16,256]{1,0:T(8,128)S(1)} %bitcast.322, f32[16,256]{1,0:T(8,128)S(1)} %bitcast.325, f32[16,256]{1,0:T(8,128)S(1)} %bitcast.328, f32[16,256]{1,0:T(8,128)S(1)} %bitcast.331, ...), kind=kLoop, calls=%fused_computation.68.clone.1 | loop fusion | flops 68153344 | bytes 376832 | tf_op jit(solution)/shard_map/while/body/eval_jaxpr/reduce_sum | solution.py:93
  1043.4 15.9 %fusion.90 = (f32[16,256]{1,0:T(8,128)S(1)}, f32[16,256]{1,0:T(8,128)S(1)}, f32[16,256]{1,0:T(8,128)S(1)}, f32[16,256]{1,0:T(8,128)S(1)}, f32[16,256]{1,0:T(8,128)S(1)}, /*index=5*/f32[16,256]{1,0:T(8,128)S(1)}) fusion(f32[16,256]{1,0:T(8,128)S(1)} %bitcast.376, f32[16,256]{1,0:T(8,128)S(1)} %bitcast.339, f32[16,256]{1,0:T(8,128)S(1)} %bitcast.342, ...), kind=kLoop, calls=%fused_computation.66.clone.1 | loop fusion | flops 79667200 | bytes 491520 | tf_op jit(solution)/shard_map/while/body/eval_jaxpr/reduce_sum | solution.py:101
  1090.8 15.9 %fusion.90 = (f32[16,256]{1,0:T(8,128)S(1)}, f32[16,256]{1,0:T(8,128)S(1)}, f32[16,256]{1,0:T(8,128)S(1)}, f32[16,256]{1,0:T(8,128)S(1)}, f32[16,256]{1,0:T(8,128)S(1)}, /*index=5*/f32[16,256]{1,0:T(8,128)S(1)}) fusion(f32[16,256]{1,0:T(8,128)S(1)} %bitcast.376, f32[16,256]{1,0:T(8,128)S(1)} %bitcast.339, f32[16,256]{1,0:T(8,128)S(1)} %bitcast.342, ...), kind=kLoop, calls=%fused_computation.66.clone.1 | loop fusion | flops 79667200 | bytes 491520 | tf_op jit(solution)/shard_map/while/body/eval_jaxpr/reduce_sum | solution.py:101
  1138.2 15.9 %fusion.90 = (f32[16,256]{1,0:T(8,128)S(1)}, f32[16,256]{1,0:T(8,128)S(1)}, f32[16,256]{1,0:T(8,128)S(1)}, f32[16,256]{1,0:T(8,128)S(1)}, f32[16,256]{1,0:T(8,128)S(1)}, /*index=5*/f32[16,256]{1,0:T(8,128)S(1)}) fusion(f32[16,256]{1,0:T(8,128)S(1)} %bitcast.376, f32[16,256]{1,0:T(8,128)S(1)} %bitcast.339, f32[16,256]{1,0:T(8,128)S(1)} %bitcast.342, ...), kind=kLoop, calls=%fused_computation.66.clone.1 | loop fusion | flops 79667200 | bytes 491520 | tf_op jit(solution)/shard_map/while/body/eval_jaxpr/reduce_sum | solution.py:101
  1185.6 15.9 %fusion.90 = (f32[16,256]{1,0:T(8,128)S(1)}, f32[16,256]{1,0:T(8,128)S(1)}, f32[16,256]{1,0:T(8,128)S(1)}, f32[16,256]{1,0:T(8,128)S(1)}, f32[16,256]{1,0:T(8,128)S(1)}, /*index=5*/f32[16,256]{1,0:T(8,128)S(1)}) fusion(f32[16,256]{1,0:T(8,128)S(1)} %bitcast.376, f32[16,256]{1,0:T(8,128)S(1)} %bitcast.339, f32[16,256]{1,0:T(8,128)S(1)} %bitcast.342, ...), kind=kLoop, calls=%fused_computation.66.clone.1 | loop fusion | flops 79667200 | bytes 491520 | tf_op jit(solution)/shard_map/while/body/eval_jaxpr/reduce_sum | solution.py:101
  1202.4 13.4 %multiply_reduce_fusion.4 = f32[16,256]{1,0:T(8,128)S(1)} fusion(f32[16,256]{1,0:T(8,128)S(1)} %bitcast.369, f32[16,256]{1,0:T(8,128)S(1)} %bitcast.371, f32[16,256]{1,0:T(8,128)S(1)} %bitcast.322, f32[16,256]{1,0:T(8,128)S(1)} %bitcast.325, f32[16,256]{1,0:T(8,128)S(1)} %bitcast.328, f32[16,256]{1,0:T(8,128)S(1)} %bitcast.331, ...), kind=kLoop, calls=%fused_computation.68.clone.1 | loop fusion | flops 68153344 | bytes 376832 | tf_op jit(solution)/shard_map/while/body/eval_jaxpr/reduce_sum | solution.py:93
  1216.2 14.0 %collective-permute-done.7 = f32[3,32,1024]{2,1,0:T(8,128)S(1)} collective-permute-done((f32[3,32,1024]{2,1,0:T(8,128)S(1)}, f32[3,32,1024]{2,1,0:T(8,128)S(1)}, u32[]{:S(2)}, u32[]{:S(2)}) %collective-permute-start.7) | collective-permute-done | bytes 393248 | tf_op jit(solution)/shard_map/ppermute | solution.py:15
  (1223 shorter events, 786.1 us)
Async XLA Ops:
  0.6 21.9 %copy-start.4 = (f32[3,64,256]{2,1,0:T(8,128)S(1)}, f32[3,64,256]{2,1,0:T(8,128)}, u32[]{:S(2)}) copy-start(f32[3,64,256]{2,1,0:T(8,128)} %param.14) | copy-start | bytes 589828
  1.7 2.7 copy-start
  2.7 1.7 copy-start.2
  3.8 0.7 copy-start.3
  4.5 16.5 %copy-start.6 = (s32[1024]{0:T(1024)}, s32[1024]{0:T(1024)S(1)}, u32[]{:S(2)}) copy-start(s32[1024]{0:T(1024)S(1)} %pad_clamp_fusion.4) | copy-start | bytes 12292
  5.3 13.1 %collective-permute-start = (f32[1,1,32,5,256]{4,3,2,1,0:T(8,128)S(1)}, f32[1,1,32,5,256]{4,3,2,1,0:T(8,128)S(1)}, u32[]{:S(2)}, u32[]{:S(2)}) collective-permute-start(f32[1,1,32,5,256]{4,3,2,1,0:T(8,128)S(1)} %bitcast.308), channel_id=1, source_target_pairs={{0,8},{8,16},{16,24},{24,32},{32,40},{40,48},{48,56},{56,64},{64,7... | collective-permute-start | bytes 491528 | tf_op jit(solution)/shard_map/ppermute | solution.py:25
  7.5 10.9 collective-permute-start.1
  14.0 7.0 copy-start.8
  14.0 7.0 copy-start.10
  18.7 8.1 collective-permute-start.2
  21.0 8.3 collective-permute-start.3
  420.6 23.1 %copy-start.7 = (s32[2,256]{1,0:T(2,128)S(1)}, s32[2,256]{1,0:T(2,128)}, u32[]{:S(2)}) copy-start(s32[2,256]{1,0:T(2,128)} %param.20) | copy-start | bytes 6148
  420.6 23.1 %copy-start.9 = (s32[64]{0:T(128)S(1)}, s32[64]{0:T(128)}, u32[]{:S(2)}) copy-start(s32[64]{0:T(128)} %copy-done.8) | copy-start | bytes 772
  420.6 23.1 %copy-start.11 = (s32[64]{0:T(128)S(1)}, s32[64]{0:T(128)}, u32[]{:S(2)}) copy-start(s32[64]{0:T(128)} %copy-done.10) | copy-start | bytes 772
  425.0 16.0 %collective-permute-start.4 = (f32[32,11,256]{2,1,0:T(8,128)S(1)}, f32[32,11,256]{2,1,0:T(8,128)S(1)}, u32[]{:S(2)}, u32[]{:S(2)}) collective-permute-start(f32[32,11,256]{2,1,0:T(8,128)S(1)} %gather_fusion.5), channel_id=1, source_target_pairs={{8,0},{16,8},{24,16},{32,24},{40,32},{48,40},{56,48},{64,56},{72,6... | collective-permute-start | bytes 1081352 | tf_op jit(solution)/shard_map/ppermute | solution.py:15
  442.4 11.2 collective-permute-start.5
  444.3 10.7 collective-permute-start.6
  455.3 2.5 copy-start.1
  457.8 774.3 %copy-start.5 = (s32[64]{0:T(128)S(1)}, s32[64]{0:T(128)}, u32[]{:S(2)}) copy-start(s32[64]{0:T(128)} %param.18) | copy-start | bytes 772
  457.8 776.9 %copy-start.12 = (s32[32]{0:T(128)S(1)}, s32[32]{0:T(128)}, u32[]{:S(2)}) copy-start(s32[32]{0:T(128)} %param.19) | copy-start | bytes 388
  1216.2 14.0 %collective-permute-start.7 = (f32[3,32,1024]{2,1,0:T(8,128)S(1)}, f32[3,32,1024]{2,1,0:T(8,128)S(1)}, u32[]{:S(2)}, u32[]{:S(2)}) collective-permute-start(f32[3,32,1024]{2,1,0:T(8,128)S(1)} %bitcast.389), channel_id=1, source_target_pairs={{120,0},{0,8},{8,16},{16,24},{24,32},{32,40},{40,48},{48,56},{56,6... | collective-permute-start | bytes 1179656 | tf_op jit(solution)/shard_map/ppermute | solution.py:15
  1230.3 4.4 collective-permute-start.8
  1231.9 2.8 collective-permute-start.9
where the time goes:
time: 1250 us; the launch traced here: 1240 us
  other arithmetic  914 us (73%)
  local copies, waits for them, and re-layouts  195 us (16%)
  matrix products  55.4 us (4%)
  waiting for transfers between devices  45.5 us (4%)
  starting transfers between devices  18.2 us (1%)
    reduce_sum x16, other arithmetic, force_block(): jnp.sum(pull_source * diff_z, axis=1)  254 us
    reduce_sum x16, other arithmetic, force_block(): jnp.sum(mass_source * (press_target + 0.5 * viscous) * work_rate, axis=2)  215 us
    reduce_sum x16, other arithmetic, force_block(): jnp.sum(mass_target * (press_source + 0.5 * viscous) * work_rate, axis=1)  200 us
    reduce_sum x24, other arithmetic, density_block(): return jnp.sum(weight * source[:, 4, None, :], axis=2)  162 us
    gather x16, local copies, waits for them, and re-layouts, force_accumulate(): source_table[source_ids]  51.2 us
    while x528, local copies, waits for them, and re-layouts  50.3 us
    dot_general x24, matrix products, density_accumulate(): jnp.dot(select, contribution, precision=lax.Precision.HIGHEST, preferred_...  38.3 us
    ppermute x6, waiting for transfers between devices, shifted(): return lax.ppermute(block, axis, route)  36.2 us
  transfers between devices with their start and end apart: 10, of which 7 were waited for; matrix products, arithmetic and copies ran while one was open for 1% of the time, Pallas kernels for 0%

commit v1 on v0

v1 whole, which is shorter than its diff:
```python
import functools
import math

import jax
import jax.numpy as jnp
from jax import lax
from jax.experimental import pallas as pl
from jax.experimental.pallas import tpu as pltpu
from jax.sharding import PartitionSpec as P

F32 = jnp.float32
SIGMA_NORM = 0.3183098861837907
GAMMA_GAS = 5.0 / 3.0
TINY = 1e-24
CELLS, SLOTS, EXPORT = 64, 256, 32
DENSITY_ROWS = 64
FORCE_ROWS = 32
VMEM, SMEM = pltpu.VMEM, pltpu.SMEM
HALF_BETA, BETA_H, SOUND, RHO, PRESS, TENTH_H = range(6)


def lanes_of(wide):
    return (0, 128) if wide else (0,)


def by_width(flag, block):
    @pl.when(flag)
    def wide_block():
        block((0, 128))

    @pl.when(jnp.logical_not(flag))
    def narrow_block():
        block((0,))


def spread(rows, target, count):
    def half(start):
        for slot, row in rows:
            part = row(start)
            target[slot, pl.ds(start, 128), :] = jnp.transpose(jnp.broadcast_to(part, (128, 128)))

    half(0)

    @pl.when(count > 128)
    def second_half():
        half(128)


def cell_row(table, cell, row):
    return lambda start: table[cell, row : row + 1, start : start + 128]


def summed_rows(values):
    return jnp.sum(values.reshape(values.shape[0] // 8, 8, 128), axis=0)


def spline_unscaled(dist_sq, smooth_twice, smooth):
    dist_sq = jnp.maximum(dist_sq, TINY)
    radius = dist_sq * lax.rsqrt(dist_sq)
    outer = jnp.maximum(smooth_twice - radius, 0.0)
    inner = jnp.maximum(smooth - radius, 0.0)
    return (0.25 * outer) * (outer * outer) - inner * (inner * inner)


def prepare_kernel(counts, exports, pos, vel, energy, masses, bins, table, near, far):
    lane = lax.broadcasted_iota(jnp.int32, (1, SLOTS), 1)
    for cell in range(CELLS):
        live = (lane < counts[cell]).astype(F32)
        one = slice(cell, cell + 1)
        for axis in range(3):
            table[cell, axis : axis + 1, :] = pos[axis, one, :]
            table[cell, 5 + axis : 6 + axis, :] = vel[axis, one, :]
        table[cell, 3:4, :] = masses[one, :] * live
        table[cell, 4:5, :] = 0.4 * jnp.exp2(bins[one, :].astype(F32) * math.log2(1.2))
        table[cell, 8:9, :] = energy[one, :]
        table[cell, 9:10, :] = live

    def gather(k, carry):
        near[k] = table[exports[k], 0:4, :]
        far[k] = table[exports[k], 4:8, :]
        return carry

    lax.fori_loop(0, EXPORT, gather, 0)


def density_local_kernel(counts, starts, listed, table, raw, held):
    raw[...] = jnp.zeros_like(raw)
    size = DENSITY_ROWS

    def per_cell(cell, carry):
        count = counts[cell]
        spread([(i, cell_row(table, cell, i)) for i in range(4)], held, count)
        trips = (count + (size - 1)) // size

        def pair(target):
            def block(lanes):
                fields = []
                for l in lanes:
                    x, y, z, h = (table[target, i : i + 1, l : l + 128] for i in (0, 1, 2, 4))
                    fields.append((x, y, z, h + h, h))

                def chunk(step, totals):
                    rows = pl.ds(pl.multiple_of(step * size, size), size)
                    sx, sy, sz, mass = (held[i, rows, :] for i in range(4))
                    result = []
                    for total, (x, y, z, h2, h1) in zip(totals, fields):
                        dx, dy, dz = x - sx, y - sy, z - sz
                        weight = spline_unscaled(dx * dx + dy * dy + dz * dz, h2, h1)
                        result.append(total + summed_rows(weight * mass))
                    return tuple(result)

                totals = lax.fori_loop(0, trips, chunk, (jnp.zeros((8, 128), F32),) * len(lanes))
                for l, total in zip(lanes, totals):
                    raw[target, :, l : l + 128] += jnp.sum(total, axis=0, keepdims=True)

            by_width(counts[target] > 128, block)

        pair(cell)
        lax.fori_loop(starts[cell], starts[cell + 1], lambda j, c: (pair(listed[j]), c)[1], 0)
        return carry

    lax.fori_loop(0, CELLS, per_cell, 0)


def density_cross_kernel(
    counts, exports, starts, listed, wide, table, partial, i0, i1, i2, i3, i5, i6, i7, i8, raw, late,
    imports, held, sums,
):
    size = DENSITY_ROWS
    for direction, block in enumerate((i0, i1, i2, i3, None, i5, i6, i7, i8)):
        if block is not None:
            imports[direction * EXPORT : (direction + 1) * EXPORT] = block[...]

    def per_cell(cell, carry):
        count = counts[cell]
        raw[cell] = partial[cell]

        @pl.when(starts[cell + 1] > starts[cell])
        def with_pairs():
            spread([(i, cell_row(table, cell, r)) for i, r in enumerate((0, 1, 2, 4))], held, count)
            trips = (count + (size - 1)) // size
            sums[...] = jnp.zeros_like(sums)

            def pair(source):
                def block(lanes):
                    fields = [
                        tuple(imports[source, i : i + 1, l : l + 128] for i in range(4)) for l in lanes
                    ]

                    def chunk(step, carry):
                        rows = pl.ds(pl.multiple_of(step * size, size), size)
                        tx, ty, tz, h1 = (held[i, rows, :] for i in range(4))
                        h2 = h1 + h1
                        total = sums[rows, :]
                        for x, y, z, mass in fields:
                            dx, dy, dz = x - tx, y - ty, z - tz
                            weight = spline_unscaled(dx * dx + dy * dy + dz * dz, h2, h1)
                            total = total + weight * mass
                        sums[rows, :] = total
                        return carry

                    lax.fori_loop(0, trips, chunk, 0)

                by_width(wide[source] > 0, block)

            lax.fori_loop(starts[cell], starts[cell + 1], lambda j, c: (pair(listed[j]), c)[1], 0)
            for l in (0, 128):
                flipped = jnp.transpose(sums[l : l + 128, :])
                raw[cell, :, l : l + 128] += jnp.sum(flipped, axis=0, keepdims=True)

        inverse = pl.reciprocal(table[cell, 4:5, :], approx=False)
        cube = inverse * inverse * inverse
        raw[cell] = raw[cell] * (SIGMA_NORM * cube * cube)
        return carry

    lax.fori_loop(0, CELLS, per_cell, 0)

    def gather(k, carry):
        cell = exports[k]
        late[k, 0:1, :] = jnp.where(table[cell, 9:10, :] > 0, raw[cell], 1.0)
        late[k, 1:2, :] = table[cell, 8:9, :]
        return carry

    lax.fori_loop(0, EXPORT, gather, 0)


def force_fields(target, cell, smooth, rho, energy):
    root = math.sqrt(1.5 * SIGMA_NORM)
    inverse = pl.reciprocal(smooth, approx=False)
    square = inverse * inverse
    target[cell, HALF_BETA : HALF_BETA + 1, :] = (0.5 * root) * (square * inverse)
    target[cell, BETA_H : BETA_H + 1, :] = root * square
    target[cell, SOUND : SOUND + 1, :] = jnp.sqrt(GAMMA_GAS * (GAMMA_GAS - 1.0) * energy) * (1.0 / 40.0)
    target[cell, RHO : RHO + 1, :] = rho * (1.0 / 200.0)
    target[cell, PRESS : PRESS + 1, :] = (GAMMA_GAS - 1.0) * energy / rho
    target[cell, TENTH_H : TENTH_H + 1, :] = 0.05 * smooth


def local_force_fields(table, raw, extra):
    def one(cell, carry):
        rho = jnp.where(table[cell, 9:10, :] > 0, raw[cell], 1.0)
        force_fields(extra, cell, table[cell, 4:5, :], rho, table[cell, 8:9, :])
        return carry

    lax.fori_loop(0, CELLS, one, 0)


def slope_part(radius, half_beta, beta_h):
    reach = half_beta * radius
    outer = jnp.maximum(beta_h - reach, 0.0)
    least = jnp.minimum(outer, reach)
    return least * (outer + (outer - least))


def force_pair(row, lane):
    dx, dy, dz = lane[0] - row[0], lane[1] - row[1], lane[2] - row[2]
    dist_sq = jnp.maximum(dx * dx + dy * dy + dz * dz, TINY)
    inverse = lax.rsqrt(dist_sq)
    radius = dist_sq * inverse
    slope = (slope_part(radius, row[6], row[7]) + slope_part(radius, lane[6], lane[7])) * inverse
    approach = (lane[3] - row[3]) * dx + (lane[4] - row[4]) * dy + (lane[5] - row[5]) * dz
    smooth = lane[11] + row[11]
    converge = (
        smooth * jnp.minimum(approach, 0.0) * pl.reciprocal(dist_sq + smooth * smooth, approx=True)
    )
    viscous = converge * (converge - (lane[8] + row[8])) * pl.reciprocal(lane[9] + row[9], approx=True)
    lane_term = lane[10] + viscous
    row_term = row[10] + viscous
    return dx, dy, dz, slope, approach, lane_term, row_term


def spread_force(table, extra, held, cell, count):
    rows = [(i, cell_row(table, cell, r)) for i, r in enumerate((0, 1, 2, 5, 6, 7))]
    rows += [(6 + i, cell_row(extra, cell, i)) for i in range(6)]
    rows += [(12, cell_row(table, cell, 3))]
    spread(rows, held, count)


def force_rows_pass(held, trips, lanes, lane_fields, add_lane, row_sums):
    size = FORCE_ROWS

    def chunk(step, totals):
        rows = pl.ds(pl.multiple_of(step * size, size), size)
        row = [held[i, rows, :] for i in range(13)]
        result = []
        row_total = None
        if row_sums is not None:
            row_total = [row_sums[i, rows, :] for i in range(4)]
        for index, lane in enumerate(lane_fields):
            dx, dy, dz, slope, approach, lane_term, row_term = force_pair(row, lane)
            common = lane_term + row_term
            weight = row[12] * slope
            pull = weight * common
            terms = (pull * dx, pull * dy, pull * dz, weight * approach * lane_term)
            result += [t + summed_rows(v) for t, v in zip(totals[4 * index :], terms)]
            if row_sums is not None:
                weight = lane[12] * slope
                pull = weight * common
                terms = (pull * dx, pull * dy, pull * dz, weight * approach * row_term)
                row_total = [t + v for t, v in zip(row_total, terms)]
        if row_sums is not None:
            for i in range(4):
                row_sums[i, rows, :] = row_total[i]
        return tuple(result)

    totals = lax.fori_loop(0, trips, chunk, (jnp.zeros((8, 128), F32),) * (4 * len(lanes)))
    for index, l in enumerate(lanes):
        add_lane(l, [jnp.sum(t, axis=0, keepdims=True) for t in totals[4 * index : 4 * index + 4]])


def add_to(sums, cell):
    def add_lane(l, parts):
        for i, part in enumerate(parts):
            sums[cell, i : i + 1, l : l + 128] += part

    return add_lane


def force_local_kernel(counts, starts, listed, table, raw, own, extra, held):
    own[...] = jnp.zeros_like(own)
    local_force_fields(table, raw, extra)

    def per_cell(cell, carry):
        count = counts[cell]
        spread_force(table, extra, held, cell, count)
        trips = (count + (FORCE_ROWS - 1)) // FORCE_ROWS

        def pair(target):
            def block(lanes):
                fields = []
                for l in lanes:
                    part = [table[target, i : i + 1, l : l + 128] for i in (0, 1, 2, 5, 6, 7)]
                    fields.append(part + [extra[target, i : i + 1, l : l + 128] for i in range(6)])
                force_rows_pass(held, trips, lanes, fields, add_to(own, target), None)

            by_width(counts[target] > 128, block)

        pair(cell)
        lax.fori_loop(starts[cell], starts[cell + 1], lambda j, c: (pair(listed[j]), c)[1], 0)
        return carry

    lax.fori_loop(0, CELLS, per_cell, 0)


def force_cross_kernel(
    counts, starts, listed, wide, table, raw, n5, n6, n7, n8, f5, f6, f7, f8, l5, l6, l7, l8,
    own, b5, b6, b7, b8, extra, near, far, late, held, row_sums, back,
):
    own[...] = jnp.zeros_like(own)
    back[...] = jnp.zeros_like(back)
    local_force_fields(table, raw, extra)
    for direction, (n, f, l) in enumerate(((n5, f5, l5), (n6, f6, l6), (n7, f7, l7), (n8, f8, l8))):
        near[direction * EXPORT : (direction + 1) * EXPORT] = n[...]
        far[direction * EXPORT : (direction + 1) * EXPORT] = f[...]

        def one(k, carry):
            slot = direction * EXPORT + k
            force_fields(late, slot, f[k, 0:1, :], l[k, 0:1, :], l[k, 1:2, :])
            return carry

        lax.fori_loop(0, EXPORT, one, 0)

    def per_cell(cell, carry):
        count = counts[cell]

        @pl.when(starts[cell + 1] > starts[cell])
        def with_pairs():
            spread_force(table, extra, held, cell, count)
            trips = (count + (FORCE_ROWS - 1)) // FORCE_ROWS
            row_sums[...] = jnp.zeros_like(row_sums)

            def pair(source):
                def block(lanes):
                    fields = []
                    for l in lanes:
                        part = [near[source, i : i + 1, l : l + 128] for i in (0, 1, 2)]
                        part += [far[source, i : i + 1, l : l + 128] for i in (1, 2, 3)]
                        part += [late[source, i : i + 1, l : l + 128] for i in range(6)]
                        fields.append(part + [near[source, 3:4, l : l + 128]])
                    force_rows_pass(held, trips, lanes, fields, add_to(back, source), row_sums)

                by_width(wide[source] > 0, block)

            lax.fori_loop(starts[cell], starts[cell + 1], lambda j, c: (pair(listed[j]), c)[1], 0)
            for i in range(4):
                for l in (0, 128):
                    flipped = jnp.transpose(row_sums[i, l : l + 128, :])
                    total = jnp.sum(flipped, axis=0, keepdims=True)
                    own[cell, i : i + 1, l : l + 128] = total if i == 3 else -total

        return carry

    lax.fori_loop(0, CELLS, per_cell, 0)
    for direction, out in enumerate((b5, b6, b7, b8)):
        out[...] = back[direction * EXPORT : (direction + 1) * EXPORT]


def finish_kernel(exports, table, raw, first, second, r0, r1, r2, density, acceleration, rate, total):
    total[...] = first[...] + second[...]

    def add(k, carry):
        total[exports[k]] += r0[k] + r1[k] + r2[k]
        return carry

    lax.fori_loop(0, EXPORT, add, 0)
    for cell in range(CELLS):
        one = slice(cell, cell + 1)
        live = table[cell, 9:10, :]
        density[one, :] = raw[cell] * live
        for axis in range(3):
            acceleration[axis, one, :] = total[cell, axis : axis + 1, :] * live
        rate[one, :] = -total[cell, 3:4, :] * live


def shape(*dims):
    return jax.ShapeDtypeStruct(dims, F32)


def call(kernel, out, scalars, arrays, scratch, flops):
    many = isinstance(out, (list, tuple))
    count = len(out) if many else 1
    specs = [pl.BlockSpec(memory_space=VMEM)] * count
    return pl.pallas_call(
        kernel,
        out_shape=out,
        in_specs=[pl.BlockSpec(memory_space=SMEM)] * len(scalars)
        + [pl.BlockSpec(memory_space=VMEM)] * len(arrays),
        out_specs=specs if many else specs[0],
        scratch_shapes=scratch,
        compiler_params=pltpu.CompilerParams(vmem_limit_bytes=40 << 20),
        cost_estimate=pl.CostEstimate(flops=flops, bytes_accessed=2 << 20, transcendentals=0),
    )(*scalars, *arrays)


def shifted(block, axis, distance):
    count = lax.axis_size(axis)
    return lax.ppermute(block, axis, [((i - distance) % count, i) for i in range(count)])


def grouped(keys, values):
    index = jnp.arange(keys.shape[0], dtype=jnp.int32)
    ahead = (keys[None, :] < keys[:, None]) | (
        (keys[None, :] == keys[:, None]) & (index[None, :] < index[:, None])
    )
    place = jnp.sum(ahead.astype(jnp.int32), axis=1)
    ordered = jnp.sum(jnp.where(place[None, :] == index[:, None], values[None, :], 0), axis=1)
    cells = jnp.arange(CELLS + 1, dtype=jnp.int32)
    starts = jnp.sum((keys[None, :] < cells[:, None]).astype(jnp.int32), axis=1)
    return starts, ordered


def body(pos, vel, energy, masses, bins, counts, exports, cross_pairs, local_pairs):
    upper = cross_pairs.shape[1] // 2
    local_starts, local_list = grouped(local_pairs[1], local_pairs[0])
    cross_starts, cross_list = grouped(cross_pairs[0], cross_pairs[1])
    upper_starts, upper_list = grouped(cross_pairs[0, :upper], cross_pairs[1, :upper] - 5 * EXPORT)
    table, near, far = call(
        prepare_kernel,
        [shape(CELLS, 16, SLOTS), shape(EXPORT, 4, SLOTS), shape(EXPORT, 4, SLOTS)],
        [counts, exports],
        [pos, vel, energy, masses, bins],
        [],
        1 << 20,
    )
    down, up = shifted(near, "gx", 1), shifted(near, "gx", -1)
    left, right = shifted(near, "yz", 1), shifted(near, "yz", -1)
    near_blocks = {
        1: down, 7: up, 3: left, 5: right,
        0: shifted(down, "yz", 1), 2: shifted(down, "yz", -1),
        6: shifted(up, "yz", 1), 8: shifted(up, "yz", -1),
    }

    def upper_blocks(block):
        above = shifted(block, "gx", -1)
        return [shifted(block, "yz", -1), shifted(above, "yz", 1), above, shifted(above, "yz", -1)]

    far_blocks = upper_blocks(far)
    partial = call(
        density_local_kernel,
        shape(CELLS, 1, SLOTS),
        [counts, local_starts, local_list],
        [table],
        [VMEM((4, SLOTS, 128), F32)],
        1 << 30,
    )
    ordered = [near_blocks[i] for i in (0, 1, 2, 3, 5, 6, 7, 8)]
    wide = jnp.concatenate(
        [b[:, 3, 128] for b in ordered[:4]]
        + [jnp.zeros((EXPORT,), F32)]
        + [b[:, 3, 128] for b in ordered[4:]]
    )
    wide = (wide > 0).astype(jnp.int32)
    raw, late = call(
        density_cross_kernel,
        [shape(CELLS, 1, SLOTS), shape(EXPORT, 2, SLOTS)],
        [counts, exports, cross_starts, cross_list, wide],
        [table, partial] + ordered,
        [VMEM((9 * EXPORT, 4, SLOTS), F32), VMEM((4, SLOTS, 128), F32), VMEM((SLOTS, 128), F32)],
        2 << 30,
    )
    late_blocks = upper_blocks(late)
    first = call(
        force_local_kernel,
        shape(CELLS, 4, SLOTS),
        [counts, local_starts, local_list],
        [table, raw],
        [VMEM((CELLS, 8, SLOTS), F32), VMEM((13, SLOTS, 128), F32)],
        3 << 30,
    )
    second, right_back, left_back, up_back, corner_back = call(
        force_cross_kernel,
        [shape(CELLS, 4, SLOTS)] + [shape(EXPORT, 4, SLOTS)] * 4,
        [counts, upper_starts, upper_list, wide[5 * EXPORT :]],
        [table, raw] + [near_blocks[i] for i in (5, 6, 7, 8)] + far_blocks + late_blocks,
        [
            VMEM((CELLS, 8, SLOTS), F32),
            VMEM((4 * EXPORT, 4, SLOTS), F32),
            VMEM((4 * EXPORT, 4, SLOTS), F32),
            VMEM((4 * EXPORT, 8, SLOTS), F32),
            VMEM((13, SLOTS, 128), F32),
            VMEM((4, SLOTS, 128), F32),
            VMEM((4 * EXPORT, 4, SLOTS), F32),
        ],
        3 << 30,
    )
    from_below = shifted(up_back, "gx", 1)
    from_right = shifted(shifted(left_back, "gx", 1), "yz", -1)
    from_left = shifted(right_back + shifted(corner_back, "gx", 1), "yz", 1)
    return call(
        finish_kernel,
        [shape(CELLS, SLOTS), shape(3, CELLS, SLOTS), shape(CELLS, SLOTS)],
        [exports],
        [table, raw, first, second, from_below, from_right, from_left],
        [VMEM((CELLS, 4, SLOTS), F32)],
        1 << 20,
    )


def solution(mesh):
    both = ("gx", "yz")
    return jax.shard_map(
        body,
        mesh=mesh,
        in_specs=(
            P(None, both, None),
            P(None, both, None),
            P(both, None),
            P(both, None),
            P(both, None),
            P(both),
            P(both),
            P(None, both),
            P(None, both),
        ),
        out_specs=(P(both, None), P(None, both, None), P(both, None)),
        check_vma=False,
    )
```

time: 1250 us -> 268 us (0.21)
  the two profiles are of different devices: /device:TPU:1 before, /device:TPU:89 now
where the time goes in v1:
time: 268 us
  Pallas kernels  222 us (83%)
  starting transfers between devices  17.9 us (7%)
  waiting for transfers between devices  16.6 us (6%)
  local copies, waits for them, and re-layouts  9.48 us (4%)
    pallas_call x6, Pallas kernels, call(): pl.pallas_call(kernel, out_shape=out, in_specs=[pl.BlockSpec(memory_space...  222 us
    ppermute x21, starting transfers between devices, shifted(): lax.ppermute(block, axis, [((i - distance) % count, i) for i in range(cou...  17.9 us
    ppermute x21, waiting for transfers between devices, shifted(): lax.ppermute(block, axis, [((i - distance) % count, i) for i in range(cou...  16.6 us
    unnamed x22, local copies, waits for them, and re-layouts  6.75 us
  transfers between devices with their start and end apart: 21, of which 7 were waited for; matrix products, arithmetic and copies ran while one was open for 1% of the time, Pallas kernels for 56%

profile of v1, /device:TPU:89, one launch (start us, length us, event | category | flops | bytes accessed | tf_op | source)
XLA Modules:
  0.0 267.5 jit_solution(12314373792968078079)
XLA Ops:
  0.6 0.9 copy-done
  1.6 0.9 copy-done.1
  2.5 0.8 copy-done.2
  3.3 0.8 copy-done.3
  4.2 0.8 copy-done.4
  5.0 0.7 copy-done.5
  5.7 0.7 copy-done.7
  6.3 1.1 shard_map.112
  7.4 0.5 collective-permute-start.9
  8.0 1.0 collective-permute-start.8
  9.1 2.2 collective-permute-start.4
  12.7 32.0 %shard_map.113.partial = f32[64,1,256]{2,1,0:T(1,128)S(1)} custom-call(s32[64]{0:T(128)S(1)} %copy-done.7, s32[65]{0:T(128)S(1)} %convert_reduce_fusion.5.starts, s32[64]{0:T(128)S(1)} %select_reduce_fusion.2.listed, f32[64,16,256]{2,1,0:T(8,128)S(1)} %get-tuple-element.13.table), custom_call_target="tpu_custom_call" | custom-call | flops 1073741824 | bytes 2097152 | tf_op jit(solution)/shard_map/pallas_call | solution.py:383
  44.7 2.2 collective-permute-start
  47.3 1.7 collective-permute-start.10
  50.0 1.4 collective-permute-start.6
  51.8 2.3 collective-permute-done.7.i8.n8
  54.1 1.1 collective-permute-start.2
  55.5 0.7 collective-permute-start.1
  56.5 2.0 collective-permute-done.2.i2
  58.8 0.6 collective-permute-done.1.i0
  59.8 0.6 copy-done.6
  60.5 47.2 %shard_map.114 = (f32[64,1,256]{2,1,0:T(1,128)S(1)}, f32[32,2,256]{2,1,0:T(2,128)S(1)}) custom-call(s32[64]{0:T(128)S(1)} %copy-done.8, s32[32]{0:T(128)S(1)} %copy-done.6, s32[65]{0:T(128)S(1)} %convert_reduce_fusion.1.starts, s32[256]{0:T(256)S(1)} %select_reduce_fusion.listed, s32[288]{0:T(512)S(1)} %compare_convert_fusion.wide, ...), custom_call_target="tpu_custom_call" | custom-call | flops 2147483648 | bytes 2097152 | tf_op jit(solution)/shard_map/pallas_call | solution.py:383
  107.9 3.1 %collective-permute-start.12 = (f32[32,2,256]{2,1,0:T(2,128)S(1)}, f32[32,2,256]{2,1,0:T(2,128)S(1)}, u32[]{:S(2)}, u32[]{:S(2)}) collective-permute-start(f32[32,2,256]{2,1,0:T(2,128)S(1)} %get-tuple-element.17), channel_id=1, source_target_pairs={{1,0},{2,1},{3,2},{4,3},{5,4},{6,5},{7,6},{0,7},{9,8},{10,9},{11,1... | collective-permute-start | bytes 196616 | tf_op jit(solution)/shard_map/ppermute | solution.py:397
  111.0 2.0 collective-permute-done.13.l7
  113.0 1.7 collective-permute-start.14
  115.0 2.0 collective-permute-done.15.l8
  117.0 69.3 %shard_map.116 = (f32[64,4,256]{2,1,0:T(4,128)S(1)}, f32[32,4,256]{2,1,0:T(4,128)S(1)}, f32[32,4,256]{2,1,0:T(4,128)S(1)}, f32[32,4,256]{2,1,0:T(4,128)S(1)}, f32[32,4,256]{2,1,0:T(4,128)S(1)}) custom-call(s32[64]{0:T(128)S(1)} %copy-done.8, s32[65]{0:T(128)S(1)} %convert_reduce_fusion.3.starts, s32[128]{0:T(128)S(1)} %select_reduce_fusion.1.listed, ...), custom_call_target="tpu_custom_call" | custom-call | flops 3221225472 | bytes 2097152 | tf_op jit(solution)/shard_map/pallas_call | solution.py:383
  186.6 4.9 %collective-permute-done.19 = f32[32,4,256]{2,1,0:T(4,128)S(1)} collective-permute-done((f32[32,4,256]{2,1,0:T(4,128)S(1)}, f32[32,4,256]{2,1,0:T(4,128)S(1)}, u32[]{:S(2)}, u32[]{:S(2)}) %collective-permute-start.19) | collective-permute-done | bytes 131104 | tf_op jit(solution)/shard_map/ppermute | solution.py:397
  191.5 2.7 %collective-permute-done.17 = f32[32,4,256]{2,1,0:T(4,128)S(1)} collective-permute-done((f32[32,4,256]{2,1,0:T(4,128)S(1)}, f32[32,4,256]{2,1,0:T(4,128)S(1)}, u32[]{:S(2)}, u32[]{:S(2)}) %collective-permute-start.17) | collective-permute-done | bytes 131104 | tf_op jit(solution)/shard_map/ppermute | solution.py:397
  194.2 1.4 collective-permute-start.18
  195.6 70.2 %shard_map.115.first = f32[64,4,256]{2,1,0:T(4,128)S(1)} custom-call(s32[64]{0:T(128)S(1)} %copy-done.8, s32[65]{0:T(128)S(1)} %convert_reduce_fusion.5.starts, s32[64]{0:T(128)S(1)} %select_reduce_fusion.2.listed, f32[64,16,256]{2,1,0:T(8,128)S(1)} %get-tuple-element.13.table, f32[64,1,256]{2,1,0:T(1,128)S(1)} %get-tuple-element.15.raw), custom_call_target="tpu_custom_call" | custom-call | flops 3221225472 | bytes 2097152 | tf_op jit(solution)/shard_map/pallas_call | solution.py:383
  265.8 1.7 shard_map.117
  (63 shorter events, 5.2 us)
Async XLA Ops:
  0.6 0.9 copy-start
  1.6 0.9 copy-start.1
  2.5 0.8 copy-start.2
  3.3 0.8 copy-start.3
  4.2 0.8 copy-start.4
  5.0 0.7 copy-start.5
  5.7 0.7 copy-start.7
  7.4 3.9 %copy-start.10 = (s32[2,64]{1,0:T(2,128)S(1)}, s32[2,64]{1,0:T(2,128)}, u32[]{:S(2)}) copy-start(s32[2,64]{1,0:T(2,128)} %param.17) | copy-start | bytes 1540
  7.4 37.3 %collective-permute-start.9 = (f32[32,4,256]{2,1,0:T(4,128)S(1)}, f32[32,4,256]{2,1,0:T(4,128)S(1)}, u32[]{:S(2)}, u32[]{:S(2)}) collective-permute-start(f32[32,4,256]{2,1,0:T(4,128)S(1)} %get-tuple-element.16), channel_id=1, source_target_pairs={{8,0},{16,8},{24,16},{32,24},{40,32},{48,40},{56,48},{64,56},{72,6... | collective-permute-start | bytes 393224 | tf_op jit(solution)/shard_map/ppermute | solution.py:397
  8.0 105.0 %collective-permute-start.8 = (f32[32,4,256]{2,1,0:T(4,128)S(1)}, f32[32,4,256]{2,1,0:T(4,128)S(1)}, u32[]{:S(2)}, u32[]{:S(2)}) collective-permute-start(f32[32,4,256]{2,1,0:T(4,128)S(1)} %get-tuple-element.16), channel_id=1, source_target_pairs={{1,0},{2,1},{3,2},{4,3},{5,4},{6,5},{7,6},{0,7},{9,8},{10,9},{11,1... | collective-permute-start | bytes 393224 | tf_op jit(solution)/shard_map/ppermute | solution.py:397
  8.9 38.0 %collective-permute-start.5 = (f32[32,4,256]{2,1,0:T(4,128)S(1)}, f32[32,4,256]{2,1,0:T(4,128)S(1)}, u32[]{:S(2)}, u32[]{:S(2)}) collective-permute-start(f32[32,4,256]{2,1,0:T(4,128)S(1)} %get-tuple-element.14), channel_id=1, source_target_pairs={{8,0},{16,8},{24,16},{32,24},{40,32},{48,40},{56,48},{64,56},{72,6... | collective-permute-start | bytes 393224 | tf_op jit(solution)/shard_map/ppermute | solution.py:397
  9.1 38.2 %collective-permute-start.4 = (f32[32,4,256]{2,1,0:T(4,128)S(1)}, f32[32,4,256]{2,1,0:T(4,128)S(1)}, u32[]{:S(2)}, u32[]{:S(2)}) collective-permute-start(f32[32,4,256]{2,1,0:T(4,128)S(1)} %get-tuple-element.14), channel_id=1, source_target_pairs={{1,0},{2,1},{3,2},{4,3},{5,4},{6,5},{7,6},{0,7},{9,8},{10,9},{11,1... | collective-permute-start | bytes 393224 | tf_op jit(solution)/shard_map/ppermute | solution.py:397
  11.3 38.1 %collective-permute-start.3 = (f32[32,4,256]{2,1,0:T(4,128)S(1)}, f32[32,4,256]{2,1,0:T(4,128)S(1)}, u32[]{:S(2)}, u32[]{:S(2)}) collective-permute-start(f32[32,4,256]{2,1,0:T(4,128)S(1)} %get-tuple-element.14), channel_id=1, source_target_pairs={{7,0},{0,1},{1,2},{2,3},{3,4},{4,5},{5,6},{6,7},{15,8},{8,9},{9,10... | collective-permute-start | bytes 393224 | tf_op jit(solution)/shard_map/ppermute | solution.py:397
  11.3 0.7 copy-start.9
  44.7 5.3 %collective-permute-start = (f32[32,4,256]{2,1,0:T(4,128)S(1)}, f32[32,4,256]{2,1,0:T(4,128)S(1)}, u32[]{:S(2)}, u32[]{:S(2)}) collective-permute-start(f32[32,4,256]{2,1,0:T(4,128)S(1)} %get-tuple-element.14), channel_id=1, source_target_pairs={{120,0},{0,8},{8,16},{16,24},{24,32},{32,40},{40,48},{48,56},{56,6... | collective-permute-start | bytes 393224 | tf_op jit(solution)/shard_map/ppermute | solution.py:397
  47.0 68.0 %collective-permute-start.11 = (f32[32,4,256]{2,1,0:T(4,128)S(1)}, f32[32,4,256]{2,1,0:T(4,128)S(1)}, u32[]{:S(2)}, u32[]{:S(2)}) collective-permute-start(f32[32,4,256]{2,1,0:T(4,128)S(1)} %collective-permute-done.9.f7), channel_id=1, source_target_pairs={{1,0},{2,1},{3,2},{4,3},{5,4},{6,5},{7,6},{0,7},{9,8},{10,9},{11,1... | collective-permute-start | bytes 393224 | tf_op jit(solution)/shard_map/ppermute | solution.py:397
  47.3 67.7 %collective-permute-start.10 = (f32[32,4,256]{2,1,0:T(4,128)S(1)}, f32[32,4,256]{2,1,0:T(4,128)S(1)}, u32[]{:S(2)}, u32[]{:S(2)}) collective-permute-start(f32[32,4,256]{2,1,0:T(4,128)S(1)} %collective-permute-done.9.f7), channel_id=1, source_target_pairs={{7,0},{0,1},{1,2},{2,3},{3,4},{4,5},{5,6},{6,7},{15,8},{8,9},{9,10... | collective-permute-start | bytes 393224 | tf_op jit(solution)/shard_map/ppermute | solution.py:397
  49.4 4.7 %collective-permute-start.7 = (f32[32,4,256]{2,1,0:T(4,128)S(1)}, f32[32,4,256]{2,1,0:T(4,128)S(1)}, u32[]{:S(2)}, u32[]{:S(2)}) collective-permute-start(f32[32,4,256]{2,1,0:T(4,128)S(1)} %collective-permute-done.5.i7.n7), channel_id=1, source_target_pairs={{1,0},{2,1},{3,2},{4,3},{5,4},{6,5},{7,6},{0,7},{9,8},{10,9},{11,1... | collective-permute-start | bytes 393224 | tf_op jit(solution)/shard_map/ppermute | solution.py:397
  50.0 5.5 %collective-permute-start.6 = (f32[32,4,256]{2,1,0:T(4,128)S(1)}, f32[32,4,256]{2,1,0:T(4,128)S(1)}, u32[]{:S(2)}, u32[]{:S(2)}) collective-permute-start(f32[32,4,256]{2,1,0:T(4,128)S(1)} %collective-permute-done.5.i7.n7), channel_id=1, source_target_pairs={{7,0},{0,1},{1,2},{2,3},{3,4},{4,5},{5,6},{6,7},{15,8},{8,9},{9,10... | collective-permute-start | bytes 393224 | tf_op jit(solution)/shard_map/ppermute | solution.py:397
  54.1 4.4 %collective-permute-start.2 = (f32[32,4,256]{2,1,0:T(4,128)S(1)}, f32[32,4,256]{2,1,0:T(4,128)S(1)}, u32[]{:S(2)}, u32[]{:S(2)}) collective-permute-start(f32[32,4,256]{2,1,0:T(4,128)S(1)} %collective-permute-done.i1), channel_id=1, source_target_pairs={{1,0},{2,1},{3,2},{4,3},{5,4},{6,5},{7,6},{0,7},{9,8},{10,9},{11,1... | collective-permute-start | bytes 393224 | tf_op jit(solution)/shard_map/ppermute | solution.py:397
  55.5 3.9 %collective-permute-start.1 = (f32[32,4,256]{2,1,0:T(4,128)S(1)}, f32[32,4,256]{2,1,0:T(4,128)S(1)}, u32[]{:S(2)}, u32[]{:S(2)}) collective-permute-start(f32[32,4,256]{2,1,0:T(4,128)S(1)} %collective-permute-done.i1), channel_id=1, source_target_pairs={{7,0},{0,1},{1,2},{2,3},{3,4},{4,5},{5,6},{6,7},{15,8},{8,9},{9,10... | collective-permute-start | bytes 393224 | tf_op jit(solution)/shard_map/ppermute | solution.py:397
  59.8 0.7 copy-start.6
  59.8 0.7 copy-start.8
  107.7 5.3 %collective-permute-start.13 = (f32[32,2,256]{2,1,0:T(2,128)S(1)}, f32[32,2,256]{2,1,0:T(2,128)S(1)}, u32[]{:S(2)}, u32[]{:S(2)}) collective-permute-start(f32[32,2,256]{2,1,0:T(2,128)S(1)} %get-tuple-element.17), channel_id=1, source_target_pairs={{8,0},{16,8},{24,16},{32,24},{40,32},{48,40},{56,48},{64,56},{72,6... | collective-permute-start | bytes 196616 | tf_op jit(solution)/shard_map/ppermute | solution.py:397
  107.9 7.0 %collective-permute-start.12 = (f32[32,2,256]{2,1,0:T(2,128)S(1)}, f32[32,2,256]{2,1,0:T(2,128)S(1)}, u32[]{:S(2)}, u32[]{:S(2)}) collective-permute-start(f32[32,2,256]{2,1,0:T(2,128)S(1)} %get-tuple-element.17), channel_id=1, source_target_pairs={{1,0},{2,1},{3,2},{4,3},{5,4},{6,5},{7,6},{0,7},{9,8},{10,9},{11,1... | collective-permute-start | bytes 196616 | tf_op jit(solution)/shard_map/ppermute | solution.py:397
  113.0 4.0 %collective-permute-start.15 = (f32[32,2,256]{2,1,0:T(2,128)S(1)}, f32[32,2,256]{2,1,0:T(2,128)S(1)}, u32[]{:S(2)}, u32[]{:S(2)}) collective-permute-start(f32[32,2,256]{2,1,0:T(2,128)S(1)} %collective-permute-done.13.l7), channel_id=1, source_target_pairs={{1,0},{2,1},{3,2},{4,3},{5,4},{6,5},{7,6},{0,7},{9,8},{10,9},{11,1... | collective-permute-start | bytes 196616 | tf_op jit(solution)/shard_map/ppermute | solution.py:397
  113.0 4.0 %collective-permute-start.14 = (f32[32,2,256]{2,1,0:T(2,128)S(1)}, f32[32,2,256]{2,1,0:T(2,128)S(1)}, u32[]{:S(2)}, u32[]{:S(2)}) collective-permute-start(f32[32,2,256]{2,1,0:T(2,128)S(1)} %collective-permute-done.13.l7), channel_id=1, source_target_pairs={{7,0},{0,1},{1,2},{2,3},{3,4},{4,5},{5,6},{6,7},{15,8},{8,9},{9,10... | collective-permute-start | bytes 196616 | tf_op jit(solution)/shard_map/ppermute | solution.py:397
  186.3 5.1 %collective-permute-start.19 = (f32[32,4,256]{2,1,0:T(4,128)S(1)}, f32[32,4,256]{2,1,0:T(4,128)S(1)}, u32[]{:S(2)}, u32[]{:S(2)}) collective-permute-start(f32[32,4,256]{2,1,0:T(4,128)S(1)} %get-tuple-element.22), channel_id=1, source_target_pairs={{120,0},{0,8},{8,16},{16,24},{24,32},{32,40},{40,48},{48,56},{56,6... | collective-permute-start | bytes 393224 | tf_op jit(solution)/shard_map/ppermute | solution.py:397
  186.4 7.8 %collective-permute-start.17 = (f32[32,4,256]{2,1,0:T(4,128)S(1)}, f32[32,4,256]{2,1,0:T(4,128)S(1)}, u32[]{:S(2)}, u32[]{:S(2)}) collective-permute-start(f32[32,4,256]{2,1,0:T(4,128)S(1)} %get-tuple-element.20), channel_id=1, source_target_pairs={{120,0},{0,8},{8,16},{16,24},{24,32},{32,40},{40,48},{48,56},{56,6... | collective-permute-start | bytes 393224 | tf_op jit(solution)/shard_map/ppermute | solution.py:397
  186.5 79.3 %collective-permute-start.16 = (f32[32,4,256]{2,1,0:T(4,128)S(1)}, f32[32,4,256]{2,1,0:T(4,128)S(1)}, u32[]{:S(2)}, u32[]{:S(2)}) collective-permute-start(f32[32,4,256]{2,1,0:T(4,128)S(1)} %get-tuple-element.19), channel_id=1, source_target_pairs={{120,0},{0,8},{8,16},{16,24},{24,32},{32,40},{40,48},{48,56},{56,6... | collective-permute-start | bytes 393224 | tf_op jit(solution)/shard_map/ppermute | solution.py:397
  191.5 74.4 %collective-permute-start.20 = (f32[32,4,256]{2,1,0:T(4,128)S(1)}, f32[32,4,256]{2,1,0:T(4,128)S(1)}, u32[]{:S(2)}, u32[]{:S(2)}) collective-permute-start(f32[32,4,256]{2,1,0:T(4,128)S(1)} %add.5), channel_id=1, source_target_pairs={{7,0},{0,1},{1,2},{2,3},{3,4},{4,5},{5,6},{6,7},{15,8},{8,9},{9,10... | collective-permute-start | bytes 393224 | tf_op jit(solution)/shard_map/ppermute | solution.py:397
  194.2 71.6 %collective-permute-start.18 = (f32[32,4,256]{2,1,0:T(4,128)S(1)}, f32[32,4,256]{2,1,0:T(4,128)S(1)}, u32[]{:S(2)}, u32[]{:S(2)}) collective-permute-start(f32[32,4,256]{2,1,0:T(4,128)S(1)} %collective-permute-done.17), channel_id=1, source_target_pairs={{1,0},{2,1},{3,2},{4,3},{5,4},{6,5},{7,6},{0,7},{9,8},{10,9},{11,1... | collective-permute-start | bytes 393224 | tf_op jit(solution)/shard_map/ppermute | solution.py:397

commit v2 on v1

v2 whole, which is shorter than its diff:
```python
import math

import jax
import jax.numpy as jnp
from jax import lax
from jax.experimental import pallas as pl
from jax.experimental.pallas import tpu as pltpu
from jax.sharding import PartitionSpec as P

F32, I32 = jnp.float32, jnp.int32
SIGMA_NORM = 0.3183098861837907
GAMMA_GAS = 5.0 / 3.0
TINY = 1e-24
CELLS, SLOTS, EXPORT = 64, 256, 32
PIECES = 2
DENSITY_ROWS = 64
FORCE_ROWS = 32
SHARE = 24
ROOT = math.sqrt(1.5 * SIGMA_NORM)
VMEM, SMEM = pltpu.VMEM, pltpu.SMEM
MESH = pl.DeviceIdType.MESH
SIDES = (0, 1, 2, 3, 5, 6, 7, 8)
FORCE_LANES = [(0, 0), (0, 1), (0, 2), (0, 5), (0, 6), (0, 7), (1, 0), (1, 1), (1, 2), (2, 0), (2, 1), (1, 3), (0, 3)]
FORCE_FAR = [(0, 0), (0, 1), (0, 2), (0, 5), (0, 6), (0, 7), (1, 0), (1, 1), (1, 2), (1, 4), (1, 5), (1, 3), (0, 3)]


def by_width(flag, block):
    @pl.when(flag)
    def wide_block():
        block((0, 128))

    @pl.when(jnp.logical_not(flag))
    def narrow_block():
        block((0,))


def flipped(row):
    return jnp.transpose(jnp.broadcast_to(row, (128, 128)))


def spread(rows, target, count, derive=None):
    def half(start):
        made = {}
        for slot, table, cell, row in rows:
            made[slot] = flipped(table[cell, row : row + 1, start : start + 128])
        if derive is not None:
            derive(made)
        for slot, value in made.items():
            target[slot, start : start + 128, :] = value

    half(0)

    @pl.when(count > 128)
    def second_half():
        half(128)


def summed_rows(values):
    return jnp.sum(values.reshape(values.shape[0] // 8, 8, 128), axis=0)


def spline_unscaled(radius, smooth_twice, smooth):
    outer = jnp.maximum(smooth_twice - radius, 0.0)
    inner = jnp.maximum(smooth - radius, 0.0)
    return (0.25 * outer) * (outer * outer) - inner * (inner * inner)


def prepare_kernel(counts, exports, pos, vel, energy, masses, bins, first, second, near, far):
    lane = lax.broadcasted_iota(I32, (1, SLOTS), 1)
    smooth = 0.4 * jnp.exp2(bins[...].astype(F32) * math.log2(1.2))
    made = derived_fields(smooth, energy[...])
    for cell in range(CELLS):
        live = (lane < counts[cell]).astype(F32)
        one = slice(cell, cell + 1)
        for axis in range(3):
            first[cell, axis : axis + 1, :] = pos[axis, one, :]
            first[cell, 5 + axis : 6 + axis, :] = vel[axis, one, :]
        first[cell, 3:4, :] = masses[one, :] * live
        first[cell, 4:5, :] = smooth[one, :]
        for i, value in enumerate(made):
            second[cell, i : i + 1, :] = value[one, :]
        second[cell, 4:5, :] = energy[one, :]
        second[cell, 5:6, :] = live

    def gather(k, carry):
        near[k] = first[exports[k]]
        far[k] = second[exports[k], 4:5, :]
        return carry

    lax.fori_loop(0, EXPORT, gather, 0)


def derived_fields(smooth, energy):
    inverse = pl.reciprocal(smooth, approx=True)
    square = inverse * inverse
    sound = jnp.sqrt(GAMMA_GAS * (GAMMA_GAS - 1.0) * energy) * (1.0 / 40.0)
    return (0.5 * ROOT) * (square * inverse), ROOT * square, sound, 0.05 * smooth


def place_of(side):
    rows, columns = lax.axis_size("gx"), lax.axis_size("yz")
    g = lax.rem(lax.axis_index("gx") + (side // 3 - 1 + rows), rows)
    y = lax.rem(lax.axis_index("yz") + (side % 3 - 1 + columns), columns)
    return g, y


def greet(sides):
    barrier = pltpu.get_barrier_semaphore()
    for side in sides:
        pl.semaphore_signal(barrier, inc=1, device_id=place_of(side), device_id_type=MESH)
    pl.semaphore_wait(barrier, len(sides))


def remote(source, target, send, receive, side):
    return pltpu.make_async_remote_copy(
        src_ref=source,
        dst_ref=target,
        send_sem=send,
        recv_sem=receive,
        device_id=place_of(side),
        device_id_type=MESH,
    )


def part_of(ref, side, piece):
    size = EXPORT // PIECES
    return ref.at[pl.ds(side * EXPORT + piece * size, size)]


def halo_kernel(near, far, note, near_all, far_all, notes, send, receive):
    greet((1, 3, 5, 7))
    kinds = [(near, near_all, p) for p in range(PIECES)] + [(far, far_all, None), (note, notes, None)]
    started = {}

    def view(ref, slot, piece):
        if piece is not None:
            return part_of(ref, slot, piece)
        size = EXPORT if ref is far_all or ref is far else 1
        return ref.at[pl.ds(slot * size, size)]

    for kind, (own, whole, piece) in enumerate(kinds):
        for side in (7, 1, 5, 3):
            slot = 8 - side
            copy = remote(view(own, 0, piece), view(whole, slot, piece), send.at[kind, slot], receive.at[kind, slot], side)
            copy.start()
            started[kind, slot] = copy
    for kind, (own, whole, piece) in enumerate(kinds):
        for came in (1, 7):
            started[kind, came].wait_recv()
            for side in (5, 3):
                slot = came + (-1 if side == 5 else 1)
                copy = remote(view(whole, came, piece), view(whole, slot, piece), send.at[kind, slot], receive.at[kind, slot], side)
                copy.start()
                started[kind, slot] = copy
    for (kind, slot), copy in started.items():
        copy.wait_send()
        if slot not in (1, 7):
            copy.wait_recv()


def swap_all(source, target, send, receive, stride):
    copies = []
    for side in SIDES:
        slot = 8 - side
        piece = source.at[pl.ds(side * EXPORT, EXPORT)] if stride else source
        copy = remote(piece, target.at[pl.ds(slot * EXPORT, EXPORT)], send.at[slot], receive.at[slot], side)
        copy.start()
        copies.append(copy)
    for copy in copies:
        copy.wait()


def total_of(block):
    parts = [block[side * EXPORT : (side + 1) * EXPORT] for side in SIDES]
    return ((parts[0] + parts[1]) + (parts[2] + parts[3])) + ((parts[4] + parts[5]) + (parts[6] + parts[7]))


def combine_kernel(exports, slot_of, first, second, partial, back, raw, late, late_all, came, sent, total, send, receive):
    greet(SIDES)
    swap_all(back, came, send.at[0], receive.at[0], True)
    total[...] = total_of(came)

    def per_cell(cell, carry):
        slot = slot_of[cell]
        extra = jnp.where(slot >= 0, total[jnp.maximum(slot, 0)], 0.0)
        inverse = pl.reciprocal(first[cell, 4:5, :], approx=True)
        cube = inverse * inverse * inverse
        value = (partial[cell] + extra) * (SIGMA_NORM * cube * cube)
        raw[cell] = value
        rho = jnp.where(second[cell, 5:6, :] > 0, value, 1.0)
        late[cell, 0:1, :] = rho * (1.0 / 200.0)
        late[cell, 1:2, :] = (GAMMA_GAS - 1.0) * second[cell, 4:5, :] * pl.reciprocal(rho, approx=True)
        return carry

    lax.fori_loop(0, CELLS, per_cell, 0)

    def gather(k, carry):
        sent[k] = late[exports[k], 0:1, :]
        return carry

    lax.fori_loop(0, EXPORT, gather, 0)
    swap_all(sent, late_all, send.at[1], receive.at[1], False)


def return_kernel(back, came, send, receive):
    greet(SIDES)
    swap_all(back, came, send, receive, True)


def lower_share(lower, upper):
    both = lower + upper
    scaled = jnp.maximum(2 * SHARE * (upper - lower) + (EXPORT + 1) * both, 0)
    return jnp.minimum(lax.div(scaled, 2 * both), EXPORT)


def set_shares(notes, shares):
    mine = notes[4, EXPORT]
    for side in SIDES:
        other = notes[side, EXPORT]
        shares[side] = lower_share(mine, other) if side > 4 else lower_share(other, mine)


def cross_loop(starts, listed, shares, notes, cell, slot, work):
    def one(j, carry):
        source = listed[j]
        side, place = source // EXPORT, source % EXPORT
        share = shares[side]
        active = jnp.where(side > 4, (place < share).astype(I32), (slot >= share).astype(I32))

        @pl.when(active > 0)
        def with_source():
            by_width(notes[side, place] > 128, lambda lanes: work(source, lanes))

        return carry

    lax.fori_loop(starts[cell], starts[cell + 1], one, 0)


def density_lanes(held, count, table, target, lanes, add_lane, lane_mass, row_sums):
    size = DENSITY_ROWS
    trips = (count + (size - 1)) // size
    fields = []
    for l in lanes:
        x, y, z, m, h = (table[target, i : i + 1, l : l + 128] for i in range(5))
        fields.append((x, y, z, m, h, h + h))

    def chunk(step, totals):
        rows = pl.ds(pl.multiple_of(step * size, size), size)
        rx, ry, rz, mass = (held[i, rows, :] for i in range(4))
        if lane_mass:
            rh = held[4, rows, :]
            rh2 = rh + rh
            row_total = row_sums[rows, :]
        result = []
        for total, (x, y, z, m, h1, h2) in zip(totals, fields):
            dx, dy, dz = x - rx, y - ry, z - rz
            dist_sq = jnp.maximum(dx * dx + dy * dy + dz * dz, TINY)
            radius = dist_sq * lax.rsqrt(dist_sq)
            result.append(total + summed_rows(spline_unscaled(radius, h2, h1) * mass))
            if lane_mass:
                row_total = row_total + spline_unscaled(radius, rh2, rh) * m
        if lane_mass:
            row_sums[rows, :] = row_total
        return tuple(result)

    totals = lax.fori_loop(0, trips, chunk, (jnp.zeros((8, 128), F32),) * len(lanes))
    for l, total in zip(lanes, totals):
        add_lane[target, :, l : l + 128] += jnp.sum(total, axis=0, keepdims=True)


def density_local(counts, starts, listed, table, raw, held, cell, count):
    def pair(target):
        by_width(
            counts[target] > 128,
            lambda lanes: density_lanes(held, count, table, target, lanes, raw, False, None),
        )

    pair(cell)
    lax.fori_loop(starts[cell], starts[cell + 1], lambda j, c: (pair(listed[j]), c)[1], 0)


def density_kernel(
    counts, slot_of, starts, listed, cross_starts, cross_list, notes, table, imports,
    raw, back, held, sums, shares,
):
    raw[...] = jnp.zeros_like(raw)
    back[...] = jnp.zeros_like(back)
    set_shares(notes, shares)

    def per_cell(cell, carry):
        count = counts[cell]
        slot = slot_of[cell]
        spread([(i, table, cell, i) for i in range(5)], held, count)
        density_local(counts, starts, listed, table, raw, held, cell, count)

        @pl.when(slot >= 0)
        def with_pairs():
            sums[...] = jnp.zeros_like(sums)
            cross_loop(
                cross_starts, cross_list, shares, notes, cell, slot,
                lambda source, lanes: density_lanes(
                    held, count, imports, source, lanes, back, True, sums
                ),
            )
            for l in (0, 128):
                turned = jnp.transpose(sums[l : l + 128, :])
                raw[cell, :, l : l + 128] += jnp.sum(turned, axis=0, keepdims=True)

        return carry

    lax.fori_loop(0, CELLS, per_cell, 0)


def slope_part(radius, half_beta, beta_h):
    reach = half_beta * radius
    outer = jnp.maximum(beta_h - reach, 0.0)
    least = jnp.minimum(outer, reach)
    return least * (outer + (outer - least))


def force_pair(row, lane):
    dx, dy, dz = lane[0] - row[0], lane[1] - row[1], lane[2] - row[2]
    dist_sq = jnp.maximum(dx * dx + dy * dy + dz * dz, TINY)
    inverse = lax.rsqrt(dist_sq)
    radius = dist_sq * inverse
    slope = (slope_part(radius, row[6], row[7]) + slope_part(radius, lane[6], lane[7])) * inverse
    approach = (lane[3] - row[3]) * dx + (lane[4] - row[4]) * dy + (lane[5] - row[5]) * dz
    smooth = lane[11] + row[11]
    converge = (
        smooth * jnp.minimum(approach, 0.0) * pl.reciprocal(dist_sq + smooth * smooth, approx=True)
    )
    viscous = converge * (converge - (lane[8] + row[8])) * pl.reciprocal(lane[9] + row[9], approx=True)
    lane_term = lane[10] + viscous
    row_term = row[10] + viscous
    return dx, dy, dz, slope, approach, lane_term, row_term


def spread_force(tables, held, cell, count):
    rows = [(i, tables[t], cell, r) for i, (t, r) in enumerate(FORCE_LANES) if i not in (6, 7, 10, 11)]
    rows.append((13, tables[0], cell, 4))

    def derive(made):
        smooth = made.pop(13)
        inverse = pl.reciprocal(smooth, approx=True)
        square = inverse * inverse
        made[7] = ROOT * square
        made[6] = (0.5 * ROOT) * (square * inverse)
        made[11] = 0.05 * smooth
        made[10] = 4.8 * (made[8] * made[8]) * pl.reciprocal(made[9], approx=True)

    spread(rows, held, count, derive)


def force_lanes(held, count, tables, target, lanes, add_lane, row_sums, places):
    size = FORCE_ROWS
    trips = (count + (size - 1)) // size
    fields = [[tables[t][target, i : i + 1, l : l + 128] for t, i in places] for l in lanes]

    def chunk(step, totals):
        rows = pl.ds(pl.multiple_of(step * size, size), size)
        row = [held[i, rows, :] for i in range(13)]
        result = []
        if row_sums is not None:
            row_total = [row_sums[i, rows, :] for i in range(4)]
        for index, lane in enumerate(fields):
            dx, dy, dz, slope, approach, lane_term, row_term = force_pair(row, lane)
            common = lane_term + row_term
            weight = row[12] * slope
            pull = weight * common
            terms = (pull * dx, pull * dy, pull * dz, weight * approach * lane_term)
            result += [t + summed_rows(v) for t, v in zip(totals[4 * index :], terms)]
            if row_sums is not None:
                weight = lane[12] * slope
                pull = weight * common
                terms = (pull * dx, pull * dy, pull * dz, weight * approach * row_term)
                row_total = [t + v for t, v in zip(row_total, terms)]
        if row_sums is not None:
            for i in range(4):
                row_sums[i, rows, :] = row_total[i]
        return tuple(result)

    totals = lax.fori_loop(0, trips, chunk, (jnp.zeros((8, 128), F32),) * (4 * len(lanes)))
    for index, l in enumerate(lanes):
        for i in range(4):
            part = jnp.sum(totals[4 * index + i], axis=0, keepdims=True)
            add_lane[target, i : i + 1, l : l + 128] += part


def force_local(counts, starts, listed, tables, own, held, cell, count):
    def pair(target):
        by_width(
            counts[target] > 128,
            lambda lanes: force_lanes(held, count, tables, target, lanes, own, None, FORCE_LANES),
        )

    pair(cell)
    lax.fori_loop(starts[cell], starts[cell + 1], lambda j, c: (pair(listed[j]), c)[1], 0)


def force_kernel(
    counts, slot_of, starts, listed, cross_starts, cross_list, notes,
    first, second, late, imports, energies, densities,
    own, back, derived, held, row_sums, shares,
):
    own[...] = jnp.zeros_like(own)
    back[...] = jnp.zeros_like(back)
    set_shares(notes, shares)
    for side in SIDES:

        def derive(step, carry):
            cells = pl.ds(side * EXPORT + step * 8, 8)
            energy = energies[cells, 0, :]
            rho = densities[cells, 0, :]
            made = derived_fields(imports[cells, 4, :], energy)
            press = (GAMMA_GAS - 1.0) / 200.0 * energy * pl.reciprocal(rho, approx=True)
            for i, value in enumerate(made + (rho, press)):
                derived[cells, i, :] = value
            return carry

        lax.fori_loop(0, EXPORT // 8, derive, 0)
    tables = (first, second, late)
    far_tables = (imports, derived)

    def per_cell(cell, carry):
        count = counts[cell]
        slot = slot_of[cell]
        spread_force(tables, held, cell, count)
        force_local(counts, starts, listed, tables, own, held, cell, count)

        @pl.when(slot >= 0)
        def with_pairs():
            row_sums[...] = jnp.zeros_like(row_sums)
            cross_loop(
                cross_starts, cross_list, shares, notes, cell, slot,
                lambda source, lanes: force_lanes(
                    held, count, far_tables, source, lanes, back, row_sums, FORCE_FAR
                ),
            )

            def finish(l):
                for i in range(4):
                    turned = jnp.transpose(row_sums[i, l : l + 128, :])
                    total = jnp.sum(turned, axis=0, keepdims=True)
                    own[cell, i : i + 1, l : l + 128] += total if i == 3 else -total

            finish(0)

            @pl.when(count > 128)
            def second_half():
                finish(128)

        return carry

    lax.fori_loop(0, CELLS, per_cell, 0)


def finish_kernel(exports, second, raw, own, came, density, acceleration, rate, extra, total):
    extra[...] = total_of(came)
    total[...] = own[...]

    def add(k, carry):
        total[exports[k]] += extra[k]
        return carry

    lax.fori_loop(0, EXPORT, add, 0)
    for cell in range(CELLS):
        one = slice(cell, cell + 1)
        live = second[cell, 5:6, :]
        density[one, :] = raw[cell] * live
        for axis in range(3):
            acceleration[axis, one, :] = total[cell, axis : axis + 1, :] * live
        rate[one, :] = -total[cell, 3:4, :] * live


def shape(*dims):
    return jax.ShapeDtypeStruct(dims, F32)


def call(kernel, out, scalars, arrays, scratch, limit=40, collective=None):
    many = isinstance(out, (list, tuple))
    count = len(out) if many else 1
    specs = [pl.BlockSpec(memory_space=VMEM)] * count
    extra = {} if collective is None else dict(collective_id=collective, has_side_effects=True)
    return pl.pallas_call(
        kernel,
        out_shape=out,
        in_specs=[pl.BlockSpec(memory_space=SMEM)] * len(scalars)
        + [pl.BlockSpec(memory_space=VMEM)] * len(arrays),
        out_specs=specs if many else specs[0],
        scratch_shapes=scratch,
        compiler_params=pltpu.CompilerParams(vmem_limit_bytes=limit << 20, **extra),
    )(*scalars, *arrays)


def grouped(keys, values):
    index = jnp.arange(keys.shape[0], dtype=I32)
    ahead = (keys[None, :] < keys[:, None]) | (
        (keys[None, :] == keys[:, None]) & (index[None, :] < index[:, None])
    )
    place = jnp.sum(ahead.astype(I32), axis=1)
    ordered = jnp.sum(jnp.where(place[None, :] == index[:, None], values[None, :], 0), axis=1)
    cells = jnp.arange(CELLS + 1, dtype=I32)
    starts = jnp.sum((keys[None, :] < cells[:, None]).astype(I32), axis=1)
    return starts, ordered


def body(pos, vel, energy, masses, bins, counts, exports, cross_pairs, local_pairs):
    cell_ids = jnp.arange(CELLS, dtype=I32)
    slots = jnp.arange(EXPORT, dtype=I32)
    is_export = exports[None, :] == cell_ids[:, None]
    load = jnp.sum(counts * counts)
    export_counts = jnp.sum(jnp.where(is_export, counts[:, None], 0), axis=0)
    note = jnp.concatenate([export_counts, jnp.broadcast_to(load, (128 - EXPORT,))])
    slot_of = jnp.sum(jnp.where(is_export, slots[None, :] + 1, 0), axis=1) - 1
    local_starts, local_list = grouped(local_pairs[1], local_pairs[0])
    cross_starts, cross_list = grouped(cross_pairs[0], cross_pairs[1])
    sems = pltpu.SemaphoreType.DMA
    first, second, near, far = call(
        prepare_kernel,
        [shape(CELLS, 8, SLOTS), shape(CELLS, 8, SLOTS), shape(EXPORT, 8, SLOTS), shape(EXPORT, 1, SLOTS)],
        [counts, exports],
        [pos, vel, energy, masses, bins],
        [],
        60,
    )
    imports, energies, notes = call(
        halo_kernel,
        [
            shape(9 * EXPORT, 8, SLOTS),
            shape(9 * EXPORT, 1, SLOTS),
            jax.ShapeDtypeStruct((9, 1, 128), I32),
        ],
        [],
        [near, far, note[None, None]],
        [sems((PIECES + 2, 9)), sems((PIECES + 2, 9))],
        40,
        0,
    )
    notes = jnp.concatenate([notes[:4, 0], note[None], notes[5:, 0]])
    lists = [local_starts, local_list, cross_starts, cross_list, notes]
    partial, back = call(
        density_kernel,
        [shape(CELLS, 1, SLOTS), shape(9 * EXPORT, 1, SLOTS)],
        [counts, slot_of] + lists,
        [first, imports],
        [VMEM((5, SLOTS, 128), F32), VMEM((SLOTS, 128), F32), SMEM((16,), I32)],
    )
    raw, late, densities = call(
        combine_kernel,
        [shape(CELLS, 1, SLOTS), shape(CELLS, 2, SLOTS), shape(9 * EXPORT, 1, SLOTS)],
        [exports, slot_of],
        [first, second, partial, back],
        [
            VMEM((9 * EXPORT, 1, SLOTS), F32),
            VMEM((EXPORT, 1, SLOTS), F32),
            VMEM((EXPORT, 1, SLOTS), F32),
            sems((2, 9)),
            sems((2, 9)),
        ],
        40,
        1,
    )
    own, back = call(
        force_kernel,
        [shape(CELLS, 4, SLOTS), shape(9 * EXPORT, 4, SLOTS)],
        [counts, slot_of] + lists,
        [first, second, late, imports, energies, densities],
        [
            VMEM((9 * EXPORT, 8, SLOTS), F32),
            VMEM((13, SLOTS, 128), F32),
            VMEM((4, SLOTS, 128), F32),
            SMEM((16,), I32),
        ],
    )
    came = call(
        return_kernel,
        shape(9 * EXPORT, 4, SLOTS),
        [],
        [back],
        [sems((9,)), sems((9,))],
        40,
        2,
    )
    return tuple(
        call(
            finish_kernel,
            [shape(CELLS, SLOTS), shape(3, CELLS, SLOTS), shape(CELLS, SLOTS)],
            [exports],
            [second, raw, own, came],
            [VMEM((EXPORT, 4, SLOTS), F32), VMEM((CELLS, 4, SLOTS), F32)],
        )
    )


def solution(mesh):
    both = ("gx", "yz")
    return jax.shard_map(
        body,
        mesh=mesh,
        in_specs=(
            P(None, both, None),
            P(None, both, None),
            P(both, None),
            P(both, None),
            P(both, None),
            P(both),
            P(both),
            P(None, both),
            P(None, both),
        ),
        out_specs=(P(both, None), P(None, both, None), P(both, None)),
        check_vma=False,
    )
```

time: 268 us -> 211 us (0.79)
  the two profiles are of different devices: /device:TPU:89 before, /device:TPU:7 now
where the time goes in v2:
time: 211 us; the launch traced here: 210 us
  Pallas kernels  201 us (95%)
  local copies, waits for them, and re-layouts  5.59 us (3%)
  other arithmetic  2.99 us (1%)
    pallas_call x7, Pallas kernels, call(): pl.pallas_call(kernel, out_shape=out, in_specs=[pl.BlockSpec(memory_space...  201 us

profile of v2, /device:TPU:7, one launch (start us, length us, event | category | flops | bytes accessed | tf_op | source)
XLA Modules:
  0.0 210.2 jit_solution(4007289672860426360)
XLA Ops:
  0.6 2.8 %shard_map.112 = (f32[64,8,256]{2,1,0:T(8,128)}, f32[64,8,256]{2,1,0:T(8,128)}, f32[32,8,256]{2,1,0:T(8,128)}, f32[32,1,256]{2,1,0:T(1,128)}) custom-call(s32[64]{0:T(128)} %counts.5, s32[32]{0:T(128)} %exports.5, f32[3,64,256]{2,1,0:T(8,128)} %pos.1, f32[3,64,256]{2,1,0:T(8,128)} %vel.1, f32[64,256]{1,0:T(8,128)} %energy.1, f32[64,256]{1,0:T(8,128)} %masses.1, ...), custom_call_target="tpu_custom_call" | custom-call | tf_op jit(solution)/shard_map/pallas_call | solution.py:484
  3.5 0.9 select_reduce_fusion.2
  4.3 0.8 slice_bitcast_fusion.2
  5.1 0.1 convert_reduce_fusion.3.starts
  5.2 0.2 convert_reduce_fusion.2
  5.4 0.1 select_reduce_fusion.1.listed
  5.5 0.8 fusion.4
  6.3 0.1 convert_reduce_fusion.1.cross_starts
  6.4 0.2 convert_reduce_fusion
  6.6 0.1 select_reduce_fusion.cross_list
  6.7 1.3 multiply_reduce_fusion
  8.0 0.6 pad_bitcast_fusion
  8.6 0.0 copy-start.3
  8.6 0.9 copy-done.3
  9.6 0.0 copy-start.4
  9.6 0.8 copy-done.4
  10.3 22.1 %shard_map.113 = (f32[288,8,256]{2,1,0:T(8,128)S(1)}, f32[288,1,256]{2,1,0:T(1,128)S(1)}, s32[9,1,128]{2,1,0:T(1,128)S(1)}) custom-call(f32[32,8,256]{2,1,0:T(8,128)S(1)} %copy-done.3, f32[32,1,256]{2,1,0:T(1,128)S(1)} %copy-done.4, s32[1,1,128]{2,1,0:T(1,128)S(1)} %get-tuple-element.40.note), custom_call_target="tpu_custom_call" | custom-call | tf_op jit(solution)/shard_map/pallas_call | solution.py:484
  32.5 0.0 copy-start.1
  32.5 1.0 copy-done.1
  33.5 0.0 copy-start.5
  33.5 0.7 copy-done.5
  34.2 0.0 copy-start
  34.2 0.0 copy-start.6
  34.2 49.8 %shard_map.114 = (f32[64,1,256]{2,1,0:T(1,128)S(1)}, f32[288,1,256]{2,1,0:T(1,128)S(1)}) custom-call(s32[64]{0:T(128)S(1)} %copy-done.5, s32[64]{0:T(128)S(1)} %broadcast_add_fusion.slot_of, s32[65]{0:T(128)S(1)} %convert_reduce_fusion.3.starts, s32[64]{0:T(128)S(1)} %select_reduce_fusion.1.listed, s32[65]{0:T(128)S(1)} %convert_reduce_fusion.1.cross_starts, ...), custom_call_target="tpu_custom_call" | custom-call | tf_op jit(solution)/shard_map/pallas_call | solution.py:484
  84.0 0.0 copy-start.2
  84.0 0.0 copy-done
  84.1 0.0 copy-done.6
  84.1 18.3 %shard_map.115 = (f32[64,1,256]{2,1,0:T(1,128)S(1)}, f32[64,2,256]{2,1,0:T(2,128)S(1)}, f32[288,1,256]{2,1,0:T(1,128)S(1)}) custom-call(s32[32]{0:T(128)S(1)} %copy-done.6, s32[64]{0:T(128)S(1)} %broadcast_add_fusion.slot_of, f32[64,8,256]{2,1,0:T(8,128)S(1)} %copy-done.1, f32[64,8,256]{2,1,0:T(8,128)S(1)} %copy-done, ...), custom_call_target="tpu_custom_call" | custom-call | tf_op jit(solution)/shard_map/pallas_call | solution.py:484
  102.3 0.0 copy-done.2
  102.4 71.6 %shard_map.116 = (f32[64,4,256]{2,1,0:T(4,128)S(1)}, f32[288,4,256]{2,1,0:T(4,128)S(1)}) custom-call(s32[64]{0:T(128)S(1)} %copy-done.5, s32[64]{0:T(128)S(1)} %broadcast_add_fusion.slot_of, s32[65]{0:T(128)S(1)} %convert_reduce_fusion.3.starts, s32[64]{0:T(128)S(1)} %select_reduce_fusion.1.listed, s32[65]{0:T(128)S(1)} %convert_reduce_fusion.1.cross_starts, ...), custom_call_target="tpu_custom_call" | custom-call | tf_op jit(solution)/shard_map/pallas_call | solution.py:484
  173.9 34.5 %shard_map.117.came = f32[288,4,256]{2,1,0:T(4,128)S(1)} custom-call(f32[288,4,256]{2,1,0:T(4,128)S(1)} %get-tuple-element.30.back), custom_call_target="tpu_custom_call" | custom-call | tf_op jit(solution)/shard_map/pallas_call | solution.py:484
  208.5 1.7 shard_map.118
  (5 shorter events, 0.0 us)
Async XLA Ops:
  8.6 1.0 copy-start.3
  9.6 0.8 copy-start.4
  32.5 1.0 copy-start.1
  33.5 0.7 copy-start.5
  34.2 49.9 %copy-start = (f32[64,8,256]{2,1,0:T(8,128)S(1)}, f32[64,8,256]{2,1,0:T(8,128)}, u32[]{:S(2)}) copy-start(f32[64,8,256]{2,1,0:T(8,128)} %get-tuple-element.17.second) | copy-start | bytes 1572868
  34.2 49.9 %copy-start.6 = (s32[32]{0:T(128)S(1)}, s32[32]{0:T(128)}, u32[]{:S(2)}) copy-start(s32[32]{0:T(128)} %exports.5) | copy-start | bytes 388
  84.0 18.3 %copy-start.2 = (f32[64,8,256]{2,1,0:T(8,128)S(1)}, f32[64,8,256]{2,1,0:T(8,128)}, u32[]{:S(2)}) copy-start(f32[64,8,256]{2,1,0:T(8,128)} %get-tuple-element.18.table.first) | copy-start | bytes 1572868

commit v3 on v2

--- a/solution.py
+++ b/solution.py
@@ -13,9 +13,11 @@
 TINY = 1e-24
 CELLS, SLOTS, EXPORT = 64, 256, 32
 PIECES = 2
+TOGETHER = 4
+COUNTS, SLOT_OF, EXPORTS, LOCAL_STARTS, LOCAL_LIST, CROSS_STARTS, CROSS_LIST = 0, 64, 128, 160, 232, 296, 368
+LOCAL_FIRST, CROSS_FIRST, PLAN_COUNTS, PLAN_SLOTS, LOCAL_TILES, CROSS_TILES, PLAN_SIZE = 0, 72, 144, 208, 272, 536, 1088
 DENSITY_ROWS = 64
 FORCE_ROWS = 32
-SHARE = 24
 ROOT = math.sqrt(1.5 * SIGMA_NORM)
 VMEM, SMEM = pltpu.VMEM, pltpu.SMEM
 MESH = pl.DeviceIdType.MESH
@@ -24,35 +26,58 @@
 FORCE_FAR = [(0, 0), (0, 1), (0, 2), (0, 5), (0, 6), (0, 7), (1, 0), (1, 1), (1, 2), (1, 4), (1, 5), (1, 3), (0, 3)]
 
 
-def by_width(flag, block):
-    @pl.when(flag)
-    def wide_block():
-        block((0, 128))
-
-    @pl.when(jnp.logical_not(flag))
-    def narrow_block():
-        block((0,))
+def over_tiles(plan, start, count, block):
+    def tile(index):
+        entry = plan[start + index]
+        return entry // 2, pl.ds(pl.multiple_of((entry % 2) * 128, 128), 128)
+
+    def two(step, carry):
+        block((tile(2 * step), tile(2 * step + 1)))
+        return carry
+
+    lax.fori_loop(0, count // 2, two, 0)
+
+    @pl.when(count % 2 == 1)
+    def last():
+        block((tile(count - 1),))
+
+
+def over_part(plan, cell, firsts, tiles, block):
+    start = plan[firsts + cell]
+    over_tiles(plan, tiles + start, plan[firsts + cell + 1] - start, block)
 
 
 def flipped(row):
     return jnp.transpose(jnp.broadcast_to(row, (128, 128)))
 
 
-def spread(rows, target, count, derive=None):
-    def half(start):
+def spread(rows, target, cells, counts, size, derive=None):
+    def half(place, cell, start):
         made = {}
-        for slot, table, cell, row in rows:
+        for slot, table, row in rows:
             made[slot] = flipped(table[cell, row : row + 1, start : start + 128])
         if derive is not None:
             derive(made)
         for slot, value in made.items():
-            target[slot, start : start + 128, :] = value
-
-    half(0)
-
-    @pl.when(count > 128)
-    def second_half():
-        half(128)
+            target[place * size + slot, start : start + 128, :] = value
+
+    for place, cell in enumerate(cells):
+        half(place, cell, 0)
+    for place, cell in enumerate(cells):
+
+        @pl.when(counts[place] > 128)
+        def second_half():
+            half(place, cell, 128)
+
+
+def over_cells(plan, lay, work):
+    def group(step, carry):
+        cells = [step * TOGETHER + i for i in range(TOGETHER)]
+        lay(cells, [plan[PLAN_COUNTS + cell] for cell in cells])
+        lax.fori_loop(0, TOGETHER, lambda i, c: (work(step * TOGETHER + i, i), c)[1], 0)
+        return carry
+
+    lax.fori_loop(0, CELLS // TOGETHER, group, 0)
 
 
 def summed_rows(values):
@@ -65,12 +90,27 @@
     return (0.25 * outer) * (outer * outer) - inner * (inner * inner)
 
 
-def prepare_kernel(counts, exports, pos, vel, energy, masses, bins, first, second, near, far):
+def prepare_kernel(ints, pos, vel, energy, masses, bins, first, second, near, far, note):
+    def measure(cell, totals):
+        count = ints[COUNTS + cell]
+        chunks = (count + (FORCE_ROWS - 1)) // FORCE_ROWS
+        tiles = 1 + (count > 128).astype(I32)
+        return totals[0] + chunks, totals[1] + tiles, totals[2] + chunks * tiles
+
+    chunks, tiles, both = lax.fori_loop(0, CELLS, measure, (0, 0, 0), unroll=8)
+    for k in range(EXPORT):
+        note[k] = ints[COUNTS + ints[EXPORTS + k]]
+    note[EXPORT] = chunks
+    note[EXPORT + 1] = tiles
+    note[EXPORT + 2] = both
+    for k in range(EXPORT + 3, 128):
+        note[k] = 0
+
     lane = lax.broadcasted_iota(I32, (1, SLOTS), 1)
     smooth = 0.4 * jnp.exp2(bins[...].astype(F32) * math.log2(1.2))
     made = derived_fields(smooth, energy[...])
     for cell in range(CELLS):
-        live = (lane < counts[cell]).astype(F32)
+        live = (lane < ints[COUNTS + cell]).astype(F32)
         one = slice(cell, cell + 1)
         for axis in range(3):
             first[cell, axis : axis + 1, :] = pos[axis, one, :]
@@ -83,8 +123,9 @@
         second[cell, 5:6, :] = live
 
     def gather(k, carry):
-        near[k] = first[exports[k]]
-        far[k] = second[exports[k], 4:5, :]
+        cell = ints[EXPORTS + k]
+        near[k] = first[cell]
+        far[k] = second[cell, 4:5, :]
         return carry
 
     lax.fori_loop(0, EXPORT, gather, 0)
@@ -127,8 +168,49 @@
     return ref.at[pl.ds(side * EXPORT + piece * size, size)]
 
 
-def halo_kernel(near, far, note, near_all, far_all, notes, send, receive):
-    greet((1, 3, 5, 7))
+def greet_lines():
+    barrier = pltpu.get_barrier_semaphore()
+    rows, columns = lax.axis_size("gx"), lax.axis_size("yz")
+    for step in range(1, rows):
+        pl.semaphore_signal(barrier, inc=1, device_id=line_place(step, 0), device_id_type=MESH)
+    for step in range(1, columns):
+        pl.semaphore_signal(barrier, inc=1, device_id=line_place(0, step), device_id_type=MESH)
+    pl.semaphore_wait(barrier, rows + columns - 2)
+
+
+def line_place(down, over):
+    rows, columns = lax.axis_size("gx"), lax.axis_size("yz")
+    return lax.rem(lax.axis_index("gx") + down, rows), lax.rem(lax.axis_index("yz") + over, columns)
+
+
+def gather_lines(every, part, steps, send, receive, place):
+    copies = []
+    for step in range(1, steps):
+        copy = pltpu.make_async_remote_copy(
+            src_ref=every.at[part],
+            dst_ref=every.at[part],
+            send_sem=send.at[step],
+            recv_sem=receive.at[step],
+            device_id=place(step),
+            device_id_type=MESH,
+        )
+        copy.start()
+        copies.append(copy)
+    return copies
+
+
+def halo_kernel(
+    near, far, note, near_all, far_all, notes, shares, every, send, receive, row_send, row_receive, column_send, column_receive
+):
+    columns = lax.axis_size("yz")
+    line = lax.axis_index("gx") * columns
+    notes[4] = note[0]
+    every[line + lax.axis_index("yz")] = note[0]
+    greet_lines()
+    mine = gather_lines(
+        every, pl.ds(line + lax.axis_index("yz"), 1), columns, column_send, column_receive,
+        lambda step: line_place(0, step),
+    )
     kinds = [(near, near_all, p) for p in range(PIECES)] + [(far, far_all, None), (note, notes, None)]
     started = {}
 
@@ -144,6 +226,12 @@
             copy = remote(view(own, 0, piece), view(whole, slot, piece), send.at[kind, slot], receive.at[kind, slot], side)
             copy.start()
             started[kind, slot] = copy
+    for copy in mine:
+        copy.wait()
+    lines = gather_lines(
+        every, pl.ds(line, columns), lax.axis_size("gx"), row_send, row_receive,
+        lambda step: line_place(step, 0),
+    )
     for kind, (own, whole, piece) in enumerate(kinds):
         for came in (1, 7):
             started[kind, came].wait_recv()
@@ -152,6 +240,9 @@
                 copy = remote(view(whole, came, piece), view(whole, slot, piece), send.at[kind, slot], receive.at[kind, slot], side)
                 copy.start()
                 started[kind, slot] = copy
+    for copy in lines:
+        copy.wait()
+    balance(every, shares)
     for (kind, slot), copy in started.items():
         copy.wait_send()
         if slot not in (1, 7):
@@ -175,13 +266,13 @@
     return ((parts[0] + parts[1]) + (parts[2] + parts[3])) + ((parts[4] + parts[5]) + (parts[6] + parts[7]))
 
 
-def combine_kernel(exports, slot_of, first, second, partial, back, raw, late, late_all, came, sent, total, send, receive):
+def combine_kernel(ints, first, second, partial, back, raw, late, late_all, came, sent, total, send, receive):
     greet(SIDES)
     swap_all(back, came, send.at[0], receive.at[0], True)
     total[...] = total_of(came)
 
     def per_cell(cell, carry):
-        slot = slot_of[cell]
+        slot = ints[SLOT_OF + cell]
         extra = jnp.where(slot >= 0, total[jnp.maximum(slot, 0)], 0.0)
         inverse = pl.reciprocal(first[cell, 4:5, :], approx=True)
         cube = inverse * inverse * inverse
@@ -195,7 +286,7 @@
     lax.fori_loop(0, CELLS, per_cell, 0)
 
     def gather(k, carry):
-        sent[k] = late[exports[k], 0:1, :]
+        sent[k] = late[ints[EXPORTS + k], 0:1, :]
         return carry
 
     lax.fori_loop(0, EXPORT, gather, 0)
@@ -207,48 +298,108 @@
     swap_all(back, came, send, receive, True)
 
 
-def lower_share(lower, upper):
-    both = lower + upper
-    scaled = jnp.maximum(2 * SHARE * (upper - lower) + (EXPORT + 1) * both, 0)
-    return jnp.minimum(lax.div(scaled, 2 * both), EXPORT)
-
-
-def set_shares(notes, shares):
-    mine = notes[4, EXPORT]
-    for side in SIDES:
-        other = notes[side, EXPORT]
-        shares[side] = lower_share(mine, other) if side > 4 else lower_share(other, mine)
-
-
-def cross_loop(starts, listed, shares, notes, cell, slot, work):
-    def one(j, carry):
-        source = listed[j]
-        side, place = source // EXPORT, source % EXPORT
-        share = shares[side]
-        active = jnp.where(side > 4, (place < share).astype(I32), (slot >= share).astype(I32))
-
-        @pl.when(active > 0)
-        def with_source():
-            by_width(notes[side, place] > 128, lambda lanes: work(source, lanes))
-
+def balance(every, shares):
+    loads = jnp.transpose(every[:, 0, :].astype(F32))
+    chunks, tiles, both = (loads[EXPORT + i : EXPORT + i + 1] for i in range(3))
+    local = 0.25 * tiles + 0.04 * both + (0.04 / CELLS) * (chunks * tiles)
+    lane = lax.broadcasted_iota(I32, (1, 128), 1)
+    columns = lax.axis_size("yz")
+    place = lax.rem(lane, columns)
+
+    def over(value, step):
+        if step == 0:
+            return value
+        inner = pltpu.roll(value, (128 - step) % 128, 1)
+        wrapped = pltpu.roll(value, (step * (columns - 1)) % 128, 1)
+        return jnp.where(place == (columns - 1 if step > 0 else 0), wrapped, inner)
+
+    def along(value, up, step):
+        moved_up = pltpu.roll(value, (128 - up * columns) % 128, 1) if up else value
+        return over(moved_up, step)
+
+    links = [(side // 3 - 1, side % 3 - 1) for side in (5, 6, 7, 8)]
+    scale = 0.043 * EXPORT / (CELLS * CELLS)
+    costs = [
+        (0.5 * scale) * (chunks * along(tiles, *link) + along(chunks, *link) * tiles) for link in links
+    ]
+    inverse = [0.1 / jnp.maximum(cost, 1e-3) for cost in costs]
+
+    def step(i, parts):
+        total = local
+        for link, cost, part in zip(links, costs, parts):
+            total = total + part * cost + along((1.0 - part) * cost, -link[0], -link[1])
+        return tuple(
+            jnp.clip(part + (along(total, *link) - total) * inv, 0.0, 1.0)
+            for link, inv, part in zip(links, inverse, parts)
+        )
+
+    parts = lax.fori_loop(0, 8, step, (jnp.full((1, 128), 0.5, F32),) * 4)
+    me = lax.axis_index("gx") * columns + lax.axis_index("yz")
+    for i, (link, part) in enumerate(zip(links, parts)):
+        count = jnp.floor(part * EXPORT + 0.5)
+        for row, value in ((i, count), (4 + i, along(count, -link[0], -link[1]))):
+            mine = jnp.sum(jnp.where(lane == me, value, 0.0), axis=1, keepdims=True)
+            shares[row : row + 1, :] = jnp.broadcast_to(mine, (1, 128)).astype(I32)
+
+
+def make_plan(ints, notes, shares, codes, plan):
+    def code(j, carry):
+        entry = ints[CROSS_LIST + j]
+        source, slot = entry & 1023, entry >> 10
+        side, place = source >> 5, source & 31
+        share = shares[jnp.where(side > 4, side - 5, 7 - side), 0]
+        use = jnp.where(side > 4, (place < share).astype(I32), (slot >= share).astype(I32))
+        codes[j] = source * 4 + use * (1 + (notes[side, 0, place] > 128).astype(I32))
         return carry
 
-    lax.fori_loop(starts[cell], starts[cell + 1], one, 0)
-
-
-def density_lanes(held, count, table, target, lanes, add_lane, lane_mass, row_sums):
+    lax.fori_loop(0, 256, code, 0, unroll=8)
+
+    def put(at, cell):
+        plan[at] = 2 * cell
+        plan[at + 1] = 2 * cell + 1
+
+    def per_cell(cell, carry):
+        local, cross = carry
+        plan[LOCAL_FIRST + cell] = local
+        plan[CROSS_FIRST + cell] = cross
+        count = ints[COUNTS + cell]
+        plan[PLAN_COUNTS + cell] = count
+        plan[PLAN_SLOTS + cell] = ints[SLOT_OF + cell]
+        put(LOCAL_TILES + local, cell)
+        local = local + 1 + (count > 128).astype(I32)
+
+        def add_local(j, at):
+            target = ints[LOCAL_LIST + j]
+            put(LOCAL_TILES + at, target)
+            return at + 1 + (ints[COUNTS + target] > 128).astype(I32)
+
+        def add_cross(j, at):
+            entry = codes[j]
+            put(CROSS_TILES + at, entry >> 2)
+            return at + (entry & 3)
+
+        local = lax.fori_loop(ints[LOCAL_STARTS + cell], ints[LOCAL_STARTS + cell + 1], add_local, local)
+        cross = lax.fori_loop(ints[CROSS_STARTS + cell], ints[CROSS_STARTS + cell + 1], add_cross, cross)
+        return local, cross
+
+    local, cross = lax.fori_loop(0, CELLS, per_cell, (0, 0))
+    plan[LOCAL_FIRST + CELLS] = local
+    plan[CROSS_FIRST + CELLS] = cross
+
+
+def density_lanes(held, base, count, table, lanes, add_lane, lane_mass, row_sums):
     size = DENSITY_ROWS
     trips = (count + (size - 1)) // size
     fields = []
-    for l in lanes:
-        x, y, z, m, h = (table[target, i : i + 1, l : l + 128] for i in range(5))
+    for cell, l in lanes:
+        x, y, z, m, h = (table[cell, i : i + 1, l] for i in range(5))
         fields.append((x, y, z, m, h, h + h))
 
     def chunk(step, totals):
         rows = pl.ds(pl.multiple_of(step * size, size), size)
-        rx, ry, rz, mass = (held[i, rows, :] for i in range(4))
+        rx, ry, rz, mass = (held[base + i, rows, :] for i in range(4))
         if lane_mass:
-            rh = held[4, rows, :]
+            rh = held[base + 4, rows, :]
             rh2 = rh + rh
             row_total = row_sums[rows, :]
         result = []
@@ -264,51 +415,48 @@
         return tuple(result)
 
     totals = lax.fori_loop(0, trips, chunk, (jnp.zeros((8, 128), F32),) * len(lanes))
-    for l, total in zip(lanes, totals):
-        add_lane[target, :, l : l + 128] += jnp.sum(total, axis=0, keepdims=True)
-
-
-def density_local(counts, starts, listed, table, raw, held, cell, count):
-    def pair(target):
-        by_width(
-            counts[target] > 128,
-            lambda lanes: density_lanes(held, count, table, target, lanes, raw, False, None),
-        )
-
-    pair(cell)
-    lax.fori_loop(starts[cell], starts[cell + 1], lambda j, c: (pair(listed[j]), c)[1], 0)
+    for (cell, l), total in zip(lanes, totals):
+        add_lane[cell, :, l] += jnp.sum(total, axis=0, keepdims=True)
 
 
 def density_kernel(
-    counts, slot_of, starts, listed, cross_starts, cross_list, notes, table, imports,
-    raw, back, held, sums, shares,
+    ints, notes, shares, table, imports, raw, back, plan, held, sums, codes,
 ):
     raw[...] = jnp.zeros_like(raw)
     back[...] = jnp.zeros_like(back)
-    set_shares(notes, shares)
-
-    def per_cell(cell, carry):
-        count = counts[cell]
-        slot = slot_of[cell]
-        spread([(i, table, cell, i) for i in range(5)], held, count)
-        density_local(counts, starts, listed, table, raw, held, cell, count)
+    make_plan(ints, notes, shares, codes, plan)
+
+    def lay(cells, sizes):
+        spread([(i, table, i) for i in range(5)], held, cells, sizes, 5)
+
+    def work(cell, place):
+        base = place * 5
+        count = plan[PLAN_COUNTS + cell]
+        slot = plan[PLAN_SLOTS + cell]
+        over_part(
+            plan, cell, LOCAL_FIRST, LOCAL_TILES,
+            lambda lanes: density_lanes(held, base, count, table, lanes, raw, False, None),
+        )
 
         @pl.when(slot >= 0)
         def with_pairs():
             sums[...] = jnp.zeros_like(sums)
-            cross_loop(
-                cross_starts, cross_list, shares, notes, cell, slot,
-                lambda source, lanes: density_lanes(
-                    held, count, imports, source, lanes, back, True, sums
-                ),
+            over_part(
+                plan, cell, CROSS_FIRST, CROSS_TILES,
+                lambda lanes: density_lanes(held, base, count, imports, lanes, back, True, sums),
             )
-            for l in (0, 128):
+
+            def finish(l):
                 turned = jnp.transpose(sums[l : l + 128, :])
                 raw[cell, :, l : l + 128] += jnp.sum(turned, axis=0, keepdims=True)
 
-        return carry
-
-    lax.fori_loop(0, CELLS, per_cell, 0)
+            finish(0)
+
+            @pl.when(count > 128)
+            def second_half():
+                finish(128)
+
+    over_cells(plan, lay, work)
 
 
 def slope_part(radius, half_beta, beta_h):
@@ -335,9 +483,9 @@
     return dx, dy, dz, slope, approach, lane_term, row_term
 
 
-def spread_force(tables, held, cell, count):
-    rows = [(i, tables[t], cell, r) for i, (t, r) in enumerate(FORCE_LANES) if i not in (6, 7, 10, 11)]
-    rows.append((13, tables[0], cell, 4))
+def spread_force(tables, held, cells, counts):
+    rows = [(i, tables[t], r) for i, (t, r) in enumerate(FORCE_LANES) if i not in (6, 7, 10, 11)]
+    rows.append((13, tables[0], 4))
 
     def derive(made):
         smooth = made.pop(13)
@@ -348,17 +496,17 @@
         made[11] = 0.05 * smooth
         made[10] = 4.8 * (made[8] * made[8]) * pl.reciprocal(made[9], approx=True)
 
-    spread(rows, held, count, derive)
-
-
-def force_lanes(held, count, tables, target, lanes, add_lane, row_sums, places):
+    spread(rows, held, cells, counts, 13, derive)
+
+
+def force_lanes(held, base, count, tables, lanes, add_lane, row_sums, places):
     size = FORCE_ROWS
     trips = (count + (size - 1)) // size
-    fields = [[tables[t][target, i : i + 1, l : l + 128] for t, i in places] for l in lanes]
+    fields = [[tables[t][cell, i : i + 1, l] for t, i in places] for cell, l in lanes]
 
     def chunk(step, totals):
         rows = pl.ds(pl.multiple_of(step * size, size), size)
-        row = [held[i, rows, :] for i in range(13)]
+        row = [held[base + i, rows, :] for i in range(13)]
         result = []
         if row_sums is not None:
             row_total = [row_sums[i, rows, :] for i in range(4)]
@@ -380,31 +528,17 @@
         return tuple(result)
 
     totals = lax.fori_loop(0, trips, chunk, (jnp.zeros((8, 128), F32),) * (4 * len(lanes)))
-    for index, l in enumerate(lanes):
+    for index, (cell, l) in enumerate(lanes):
         for i in range(4):
             part = jnp.sum(totals[4 * index + i], axis=0, keepdims=True)
-            add_lane[target, i : i + 1, l : l + 128] += part
-
-
-def force_local(counts, starts, listed, tables, own, held, cell, count):
-    def pair(target):
-        by_width(
-            counts[target] > 128,
-            lambda lanes: force_lanes(held, count, tables, target, lanes, own, None, FORCE_LANES),
-        )
-
-    pair(cell)
-    lax.fori_loop(starts[cell], starts[cell + 1], lambda j, c: (pair(listed[j]), c)[1], 0)
+            add_lane[cell, i : i + 1, l] += part
 
 
 def force_kernel(
-    counts, slot_of, starts, listed, cross_starts, cross_list, notes,
-    first, second, late, imports, energies, densities,
-    own, back, derived, held, row_sums, shares,
+    plan, first, second, late, imports, energies, densities, own, back, derived, held, row_sums,
 ):
     own[...] = jnp.zeros_like(own)
     back[...] = jnp.zeros_like(back)
-    set_shares(notes, shares)
     for side in SIDES:
 
         def derive(step, carry):
@@ -421,20 +555,24 @@
     tables = (first, second, late)
     far_tables = (imports, derived)
 
-    def per_cell(cell, carry):
-        count = counts[cell]
-        slot = slot_of[cell]
-        spread_force(tables, held, cell, count)
-        force_local(counts, starts, listed, tables, own, held, cell, count)
+    def lay(cells, sizes):
+        spread_force(tables, held, cells, sizes)
+
+    def work(cell, place):
+        base = place * 13
+        count = plan[PLAN_COUNTS + cell]
+        slot = plan[PLAN_SLOTS + cell]
+        over_part(
+            plan, cell, LOCAL_FIRST, LOCAL_TILES,
+            lambda lanes: force_lanes(held, base, count, tables, lanes, own, None, FORCE_LANES),
+        )
 
         @pl.when(slot >= 0)
         def with_pairs():
             row_sums[...] = jnp.zeros_like(row_sums)
-            cross_loop(
-                cross_starts, cross_list, shares, notes, cell, slot,
-                lambda source, lanes: force_lanes(
-                    held, count, far_tables, source, lanes, back, row_sums, FORCE_FAR
-                ),
+            over_part(
+                plan, cell, CROSS_FIRST, CROSS_TILES,
+                lambda lanes: force_lanes(held, base, count, far_tables, lanes, back, row_sums, FORCE_FAR),
             )
 
             def finish(l):
@@ -449,17 +587,15 @@
             def second_half():
                 finish(128)
 
-        return carry
-
-    lax.fori_loop(0, CELLS, per_cell, 0)
-
-
-def finish_kernel(exports, second, raw, own, came, density, acceleration, rate, extra, total):
+    over_cells(plan, lay, work)
+
+
+def finish_kernel(ints, second, raw, own, came, density, acceleration, rate, extra, total):
     extra[...] = total_of(came)
     total[...] = own[...]
 
     def add(k, carry):
-        total[exports[k]] += extra[k]
+        total[ints[EXPORTS + k]] += extra[k]
         return carry
 
     lax.fori_loop(0, EXPORT, add, 0)
@@ -479,7 +615,10 @@
 def call(kernel, out, scalars, arrays, scratch, limit=40, collective=None):
     many = isinstance(out, (list, tuple))
     count = len(out) if many else 1
-    specs = [pl.BlockSpec(memory_space=VMEM)] * count
+    kinds = [o.dtype for o in out] if many else [out.dtype]
+    specs = [
+        pl.BlockSpec(memory_space=SMEM if k == I32 and collective is None else VMEM) for k in kinds
+    ]
     extra = {} if collective is None else dict(collective_id=collective, has_side_effects=True)
     return pl.pallas_call(
         kernel,
@@ -508,47 +647,49 @@
     cell_ids = jnp.arange(CELLS, dtype=I32)
     slots = jnp.arange(EXPORT, dtype=I32)
     is_export = exports[None, :] == cell_ids[:, None]
-    load = jnp.sum(counts * counts)
-    export_counts = jnp.sum(jnp.where(is_export, counts[:, None], 0), axis=0)
-    note = jnp.concatenate([export_counts, jnp.broadcast_to(load, (128 - EXPORT,))])
     slot_of = jnp.sum(jnp.where(is_export, slots[None, :] + 1, 0), axis=1) - 1
     local_starts, local_list = grouped(local_pairs[1], local_pairs[0])
-    cross_starts, cross_list = grouped(cross_pairs[0], cross_pairs[1])
+    target_slot = jnp.sum(jnp.where(cross_pairs[0][:, None] == exports[None, :], slots[None, :], 0), axis=1)
+    cross_starts, cross_list = grouped(cross_pairs[0], cross_pairs[1] + 1024 * target_slot)
+    pad = jnp.zeros((7,), I32)
+    ints = jnp.concatenate(
+        [counts, slot_of, exports, local_starts, pad, local_list, cross_starts, pad, cross_list]
+    )
     sems = pltpu.SemaphoreType.DMA
-    first, second, near, far = call(
+    first, second, near, far, note = call(
         prepare_kernel,
-        [shape(CELLS, 8, SLOTS), shape(CELLS, 8, SLOTS), shape(EXPORT, 8, SLOTS), shape(EXPORT, 1, SLOTS)],
-        [counts, exports],
+        [shape(CELLS, 8, SLOTS), shape(CELLS, 8, SLOTS), shape(EXPORT, 8, SLOTS), shape(EXPORT, 1, SLOTS),
+         jax.ShapeDtypeStruct((128,), I32)],
+        [ints],
         [pos, vel, energy, masses, bins],
         [],
         60,
     )
-    imports, energies, notes = call(
+    imports, energies, notes, shares = call(
         halo_kernel,
         [
             shape(9 * EXPORT, 8, SLOTS),
             shape(9 * EXPORT, 1, SLOTS),
             jax.ShapeDtypeStruct((9, 1, 128), I32),
+            jax.ShapeDtypeStruct((8, 128), I32),
         ],
         [],
         [near, far, note[None, None]],
-        [sems((PIECES + 2, 9)), sems((PIECES + 2, 9))],
+        [VMEM((128, 1, 128), I32)] + [sems(d) for d in ((PIECES + 2, 9),) * 2 + ((16,),) * 2 + ((8,),) * 2],
         40,
         0,
     )
-    notes = jnp.concatenate([notes[:4, 0], note[None], notes[5:, 0]])
-    lists = [local_starts, local_list, cross_starts, cross_list, notes]
-    partial, back = call(
+    partial, back, plan = call(
         density_kernel,
-        [shape(CELLS, 1, SLOTS), shape(9 * EXPORT, 1, SLOTS)],
-        [counts, slot_of] + lists,
+        [shape(CELLS, 1, SLOTS), shape(9 * EXPORT, 1, SLOTS), jax.ShapeDtypeStruct((PLAN_SIZE,), I32)],
+        [ints, notes, shares],
         [first, imports],
-        [VMEM((5, SLOTS, 128), F32), VMEM((SLOTS, 128), F32), SMEM((16,), I32)],
+        [VMEM((5 * TOGETHER, SLOTS, 128), F32), VMEM((SLOTS, 128), F32), SMEM((256,), I32)],
     )
     raw, late, densities = call(
         combine_kernel,
         [shape(CELLS, 1, SLOTS), shape(CELLS, 2, SLOTS), shape(9 * EXPORT, 1, SLOTS)],
-        [exports, slot_of],
+        [ints],
         [first, second, partial, back],
         [
             VMEM((9 * EXPORT, 1, SLOTS), F32),
@@ -563,13 +704,12 @@
     own, back = call(
         force_kernel,
         [shape(CELLS, 4, SLOTS), shape(9 * EXPORT, 4, SLOTS)],
-        [counts, slot_of] + lists,
+        [plan],
         [first, second, late, imports, energies, densities],
         [
             VMEM((9 * EXPORT, 8, SLOTS), F32),
-            VMEM((13, SLOTS, 128), F32),
+            VMEM((13 * TOGETHER, SLOTS, 128), F32),
             VMEM((4, SLOTS, 128), F32),
-            SMEM((16,), I32),
         ],
     )
     came = call(
@@ -585,7 +725,7 @@
         call(
             finish_kernel,
             [shape(CELLS, SLOTS), shape(3, CELLS, SLOTS), shape(CELLS, SLOTS)],
-            [exports],
+            [ints],
             [second, raw, own, came],
             [VMEM((EXPORT, 4, SLOTS), F32), VMEM((CELLS, 4, SLOTS), F32)],
         )

time: 211 us -> 207 us (0.981)
  the two profiles are of different devices: /device:TPU:7 before, /device:TPU:1 now
where the time goes in v3:
time: 207 us; the launch traced here: 206 us
  Pallas kernels  195 us (94%)
  local copies, waits for them, and re-layouts  6.89 us (3%)
  other arithmetic  3 us (1%)
    pallas_call x7, Pallas kernels, call(): pl.pallas_call(kernel, out_shape=out, in_specs=[pl.BlockSpec(memory_space...  195 us

profile of v3, /device:TPU:1, one launch (start us, length us, event | category | flops | bytes accessed | tf_op | source)
XLA Modules:
  0.0 205.8 jit_solution(15969130980477346879)
XLA Ops:
  0.6 0.7 select_reduce_fusion.3
  1.4 0.8 slice_bitcast_fusion
  2.2 0.1 convert_reduce_fusion.3
  2.2 0.2 convert_reduce_fusion.2
  2.4 0.1 select_reduce_fusion.2
  2.5 0.7 slice.15
  3.2 0.1 convert_reduce_fusion.1
  3.4 0.8 select_reduce_fusion.1
  4.1 0.7 slice_add_fusion
  4.8 0.2 convert_reduce_fusion
  5.0 0.1 select_reduce_fusion
  5.1 1.3 concatenate.3.ints
  6.5 3.3 %shard_map.112 = (f32[64,8,256]{2,1,0:T(8,128)}, f32[64,8,256]{2,1,0:T(8,128)}, f32[32,8,256]{2,1,0:T(8,128)}, f32[32,1,256]{2,1,0:T(1,128)}, s32[128]{0:T(128)}) custom-call(s32[624]{0:T(1024)} %concatenate.3.ints, f32[3,64,256]{2,1,0:T(8,128)} %pos.1, f32[3,64,256]{2,1,0:T(8,128)} %vel.1, f32[64,256]{1,0:T(8,128)} %energy.1, f32[64,256]{1,0:T(8,128)} %masses.1, ...), custom_call_target="tpu_custom_call" | custom-call | tf_op jit(solution)/shard_map/pallas_call | solution.py:623
  9.8 0.0 copy-start.3
  9.8 0.9 copy-done.3
  10.8 0.0 copy-start.6
  10.8 0.8 copy-done.6
  11.5 0.7 copy-done.7
  12.2 24.6 %shard_map.113 = (f32[288,8,256]{2,1,0:T(8,128)S(1)}, f32[288,1,256]{2,1,0:T(1,128)S(1)}, s32[9,1,128]{2,1,0:T(1,128)S(1)}, s32[8,128]{1,0:T(8,128)S(1)}) custom-call(f32[32,8,256]{2,1,0:T(8,128)S(1)} %copy-done.3, f32[32,1,256]{2,1,0:T(1,128)S(1)} %copy-done.6, s32[1,1,128]{2,1,0:T(1,128)S(1)} %bitcast.8), custom_call_target="tpu_custom_call" | custom-call | tf_op jit(solution)/shard_map/pallas_call | solution.py:623
  36.8 0.0 copy-start
  36.8 1.0 copy-done
  37.8 0.7 copy-done.4
  38.5 48.7 %shard_map.114 = (f32[64,1,256]{2,1,0:T(1,128)S(1)}, f32[288,1,256]{2,1,0:T(1,128)S(1)}, s32[1088]{0:T(1024)S(1)}) custom-call(s32[624]{0:T(1024)S(1)} %copy-done.4, s32[9,1,128]{2,1,0:T(1,128)S(1)} %get-tuple-element.25.notes, s32[8,128]{1,0:T(8,128)S(1)} %get-tuple-element.26.shares, f32[64,8,256]{2,1,0:T(8,128)S(1)} %copy-done, ...), custom_call_target="tpu_custom_call" | custom-call | tf_op jit(solution)/shard_map/pallas_call | solution.py:623
  87.2 0.0 copy-start.1
  87.2 0.0 copy-done.2
  87.3 21.0 %shard_map.115 = (f32[64,1,256]{2,1,0:T(1,128)S(1)}, f32[64,2,256]{2,1,0:T(2,128)S(1)}, f32[288,1,256]{2,1,0:T(1,128)S(1)}) custom-call(s32[624]{0:T(1024)S(1)} %copy-done.4, f32[64,8,256]{2,1,0:T(8,128)S(1)} %copy-done, f32[64,8,256]{2,1,0:T(8,128)S(1)} %copy-done.2, f32[64,1,256]{2,1,0:T(1,128)S(1)} %get-tuple-element.28.partial, ...), custom_call_target="tpu_custom_call" | custom-call | tf_op jit(solution)/shard_map/pallas_call | solution.py:623
  108.2 0.0 copy-done.1
  108.2 75.8 %shard_map.116 = (f32[64,4,256]{2,1,0:T(4,128)S(1)}, f32[288,4,256]{2,1,0:T(4,128)S(1)}) custom-call(s32[1088]{0:T(1024)S(1)} %get-tuple-element.31.plan, f32[64,8,256]{2,1,0:T(8,128)S(1)} %copy-done.1, f32[64,8,256]{2,1,0:T(8,128)S(1)} %copy-done.2, f32[64,2,256]{2,1,0:T(2,128)S(1)} %get-tuple-element.32.late, ...), custom_call_target="tpu_custom_call" | custom-call | tf_op jit(solution)/shard_map/pallas_call | solution.py:623
  184.1 0.0 copy-start.5
  184.1 19.9 %shard_map.117.came = f32[288,4,256]{2,1,0:T(4,128)S(1)} custom-call(f32[288,4,256]{2,1,0:T(4,128)S(1)} %get-tuple-element.36.back), custom_call_target="tpu_custom_call" | custom-call | tf_op jit(solution)/shard_map/pallas_call | solution.py:623
  204.0 0.0 copy-done.5
  204.0 1.8 shard_map.118
  (7 shorter events, 0.0 us)
Async XLA Ops:
  9.8 1.0 copy-start.3
  10.8 0.8 copy-start.6
  11.5 0.7 copy-start.7
  36.8 1.0 copy-start
  37.8 0.7 copy-start.4
  38.5 48.8 %copy-start.2 = (f32[64,8,256]{2,1,0:T(8,128)S(1)}, f32[64,8,256]{2,1,0:T(8,128)}, u32[]{:S(2)}) copy-start(f32[64,8,256]{2,1,0:T(8,128)} %get-tuple-element.20.second) | copy-start | bytes 1572868
  87.2 21.0 %copy-start.1 = (f32[64,8,256]{2,1,0:T(8,128)S(1)}, f32[64,8,256]{2,1,0:T(8,128)}, u32[]{:S(2)}) copy-start(f32[64,8,256]{2,1,0:T(8,128)} %get-tuple-element.21.table.first) | copy-start | bytes 1572868
  184.1 19.9 %copy-start.5 = (s32[624]{0:T(1024)S(1)}, s32[624]{0:T(1024)}, u32[]{:S(2)}) copy-start(s32[624]{0:T(1024)} %concatenate.3.ints) | copy-start | bytes 7492

commit v4 on v3

--- a/solution.py
+++ b/solution.py
@@ -12,15 +12,17 @@
 GAMMA_GAS = 5.0 / 3.0
 TINY = 1e-24
 CELLS, SLOTS, EXPORT = 64, 256, 32
-PIECES = 2
-TOGETHER = 4
+PIECES = 4
+TOGETHER = 8
 COUNTS, SLOT_OF, EXPORTS, LOCAL_STARTS, LOCAL_LIST, CROSS_STARTS, CROSS_LIST = 0, 64, 128, 160, 232, 296, 368
 LOCAL_FIRST, CROSS_FIRST, PLAN_COUNTS, PLAN_SLOTS, LOCAL_TILES, CROSS_TILES, PLAN_SIZE = 0, 72, 144, 208, 272, 536, 1088
-DENSITY_ROWS = 64
+DENSITY_ROWS = 32
 FORCE_ROWS = 32
 ROOT = math.sqrt(1.5 * SIGMA_NORM)
 VMEM, SMEM = pltpu.VMEM, pltpu.SMEM
 MESH = pl.DeviceIdType.MESH
+DENSITY_PICKED, DENSITY_TURNED = (0, 1, 2, 3), (4,)
+FORCE_PICKED = (0, 1, 2, 3, 4, 5, 12)
 SIDES = (0, 1, 2, 3, 5, 6, 7, 8)
 FORCE_LANES = [(0, 0), (0, 1), (0, 2), (0, 5), (0, 6), (0, 7), (1, 0), (1, 1), (1, 2), (2, 0), (2, 1), (1, 3), (0, 3)]
 FORCE_FAR = [(0, 0), (0, 1), (0, 2), (0, 5), (0, 6), (0, 7), (1, 0), (1, 1), (1, 2), (1, 4), (1, 5), (1, 3), (0, 3)]
@@ -51,9 +53,34 @@
     return jnp.transpose(jnp.broadcast_to(row, (128, 128)))
 
 
-def spread(rows, target, cells, counts, size, derive=None):
+def split(values):
+    high = values.astype(jnp.bfloat16)
+    rest = values - high.astype(F32)
+    middle = rest.astype(jnp.bfloat16)
+    return high, middle, (rest - middle.astype(F32)).astype(jnp.bfloat16)
+
+
+def picker(rows):
+    width = 128 * len(rows)
+    part = lax.rem(lax.broadcasted_iota(I32, (32, width), 0), 8)
+    inside = lax.broadcasted_iota(I32, (32, width), 0) < 24
+    block = lax.broadcasted_iota(I32, (32, width), 1) // 128
+    wanted = jnp.zeros((32, width), I32)
+    for i, row in enumerate(rows):
+        wanted = jnp.where(block == i, row, wanted)
+    return jnp.where(inside & (part == wanted), 1.0, 0.0).astype(jnp.bfloat16)
+
+
+def spread(rows, target, cells, counts, size, table8, picked, pick, derive=None):
     def half(place, cell, start):
         made = {}
+        parts = split(table8[cell, :, start : start + 128])
+        left = jnp.concatenate(parts + (jnp.zeros((8, 128), jnp.bfloat16),), axis=0)
+        spreads = lax.dot_general(
+            left, pick[...], (((0,), (0,)), ((), ())), preferred_element_type=F32
+        )
+        for i, slot in enumerate(picked):
+            made[slot] = spreads[:, 128 * i : 128 * i + 128]
         for slot, table, row in rows:
             made[slot] = flipped(table[cell, row : row + 1, start : start + 128])
         if derive is not None:
@@ -128,7 +155,7 @@
         far[k] = second[cell, 4:5, :]
         return carry
 
-    lax.fori_loop(0, EXPORT, gather, 0)
+    lax.fori_loop(0, EXPORT, gather, 0, unroll=8)
 
 
 def derived_fields(smooth, energy):
@@ -283,13 +310,13 @@
         late[cell, 1:2, :] = (GAMMA_GAS - 1.0) * second[cell, 4:5, :] * pl.reciprocal(rho, approx=True)
         return carry
 
-    lax.fori_loop(0, CELLS, per_cell, 0)
+    lax.fori_loop(0, CELLS, per_cell, 0, unroll=8)
 
     def gather(k, carry):
         sent[k] = late[ints[EXPORTS + k], 0:1, :]
         return carry
 
-    lax.fori_loop(0, EXPORT, gather, 0)
+    lax.fori_loop(0, EXPORT, gather, 0, unroll=8)
     swap_all(sent, late_all, send.at[1], receive.at[1], False)
 
 
@@ -345,7 +372,7 @@
 def make_plan(ints, notes, shares, codes, plan):
     def code(j, carry):
         entry = ints[CROSS_LIST + j]
-        source, slot = entry & 1023, entry >> 10
+        source, slot = entry & 1023, ints[SLOT_OF + (entry >> 10)]
         side, place = source >> 5, source & 31
         share = shares[jnp.where(side > 4, side - 5, 7 - side), 0]
         use = jnp.where(side > 4, (place < share).astype(I32), (slot >= share).astype(I32))
@@ -420,14 +447,15 @@
 
 
 def density_kernel(
-    ints, notes, shares, table, imports, raw, back, plan, held, sums, codes,
+    ints, notes, shares, table, imports, raw, back, plan, held, sums, codes, pick,
 ):
     raw[...] = jnp.zeros_like(raw)
     back[...] = jnp.zeros_like(back)
     make_plan(ints, notes, shares, codes, plan)
+    pick[...] = picker(DENSITY_PICKED)
 
     def lay(cells, sizes):
-        spread([(i, table, i) for i in range(5)], held, cells, sizes, 5)
+        spread([(i, table, i) for i in DENSITY_TURNED], held, cells, sizes, 5, table, DENSITY_PICKED, pick)
 
     def work(cell, place):
         base = place * 5
@@ -483,8 +511,8 @@
     return dx, dy, dz, slope, approach, lane_term, row_term
 
 
-def spread_force(tables, held, cells, counts):
-    rows = [(i, tables[t], r) for i, (t, r) in enumerate(FORCE_LANES) if i not in (6, 7, 10, 11)]
+def spread_force(tables, held, cells, counts, pick):
+    rows = [(i, tables[t], r) for i, (t, r) in enumerate(FORCE_LANES) if i not in (6, 7, 10, 11) + FORCE_PICKED]
     rows.append((13, tables[0], 4))
 
     def derive(made):
@@ -496,7 +524,7 @@
         made[11] = 0.05 * smooth
         made[10] = 4.8 * (made[8] * made[8]) * pl.reciprocal(made[9], approx=True)
 
-    spread(rows, held, cells, counts, 13, derive)
+    spread(rows, held, cells, counts, 13, tables[0], FORCE_PICKED, pick, derive)
 
 
 def force_lanes(held, base, count, tables, lanes, add_lane, row_sums, places):
@@ -535,7 +563,7 @@
 
 
 def force_kernel(
-    plan, first, second, late, imports, energies, densities, own, back, derived, held, row_sums,
+    plan, first, second, late, imports, energies, densities, own, back, derived, held, row_sums, pick,
 ):
     own[...] = jnp.zeros_like(own)
     back[...] = jnp.zeros_like(back)
@@ -552,11 +580,12 @@
             return carry
 
         lax.fori_loop(0, EXPORT // 8, derive, 0)
+    pick[...] = picker([FORCE_LANES[i][1] for i in FORCE_PICKED])
     tables = (first, second, late)
     far_tables = (imports, derived)
 
     def lay(cells, sizes):
-        spread_force(tables, held, cells, sizes)
+        spread_force(tables, held, cells, sizes, pick)
 
     def work(cell, place):
         base = place * 13
@@ -598,7 +627,7 @@
         total[ints[EXPORTS + k]] += extra[k]
         return carry
 
-    lax.fori_loop(0, EXPORT, add, 0)
+    lax.fori_loop(0, EXPORT, add, 0, unroll=4)
     for cell in range(CELLS):
         one = slice(cell, cell + 1)
         live = second[cell, 5:6, :]
@@ -649,8 +678,7 @@
     is_export = exports[None, :] == cell_ids[:, None]
     slot_of = jnp.sum(jnp.where(is_export, slots[None, :] + 1, 0), axis=1) - 1
     local_starts, local_list = grouped(local_pairs[1], local_pairs[0])
-    target_slot = jnp.sum(jnp.where(cross_pairs[0][:, None] == exports[None, :], slots[None, :], 0), axis=1)
-    cross_starts, cross_list = grouped(cross_pairs[0], cross_pairs[1] + 1024 * target_slot)
+    cross_starts, cross_list = grouped(cross_pairs[0], cross_pairs[1] + 1024 * cross_pairs[0])
     pad = jnp.zeros((7,), I32)
     ints = jnp.concatenate(
         [counts, slot_of, exports, local_starts, pad, local_list, cross_starts, pad, cross_list]
@@ -684,7 +712,8 @@
         [shape(CELLS, 1, SLOTS), shape(9 * EXPORT, 1, SLOTS), jax.ShapeDtypeStruct((PLAN_SIZE,), I32)],
         [ints, notes, shares],
         [first, imports],
-        [VMEM((5 * TOGETHER, SLOTS, 128), F32), VMEM((SLOTS, 128), F32), SMEM((256,), I32)],
+        [VMEM((5 * TOGETHER, SLOTS, 128), F32), VMEM((SLOTS, 128), F32), SMEM((256,), I32),
+         VMEM((32, 128 * len(DENSITY_PICKED)), jnp.bfloat16)],
     )
     raw, late, densities = call(
         combine_kernel,
@@ -710,6 +739,7 @@
             VMEM((9 * EXPORT, 8, SLOTS), F32),
             VMEM((13 * TOGETHER, SLOTS, 128), F32),
             VMEM((4, SLOTS, 128), F32),
+            VMEM((32, 128 * len(FORCE_PICKED)), jnp.bfloat16),
         ],
     )
     came = call(

time: 207 us -> 191 us (0.923)
  the two profiles are of different devices: /device:TPU:1 before, /device:TPU:67 now
where the time goes in v4:
time: 191 us
  Pallas kernels  182 us (95%)
  local copies, waits for them, and re-layouts  6.2 us (3%)
  other arithmetic  2.33 us (1%)
    pallas_call x7, Pallas kernels, call(): pl.pallas_call(kernel, out_shape=out, in_specs=[pl.BlockSpec(memory_space...  182 us
    unnamed x16, local copies, waits for them, and re-layouts  4.09 us

profile of v4, /device:TPU:67, one launch (start us, length us, event | category | flops | bytes accessed | tf_op | source)
XLA Modules:
  0.0 191.0 jit_solution(14875282233768634265)
XLA Ops:
  0.6 0.7 select_reduce_fusion.2
  1.4 0.8 slice_bitcast_fusion
  2.2 0.1 convert_reduce_fusion.3
  2.2 0.2 convert_reduce_fusion.2
  2.4 0.1 select_reduce_fusion.1
  2.5 0.8 multiply_add_fusion
  3.3 0.1 convert_reduce_fusion.1
  3.4 0.2 convert_reduce_fusion
  3.6 0.1 select_reduce_fusion
  3.8 1.3 concatenate.3.ints
  5.1 3.2 %shard_map.112 = (f32[64,8,256]{2,1,0:T(8,128)}, f32[64,8,256]{2,1,0:T(8,128)}, f32[32,8,256]{2,1,0:T(8,128)}, f32[32,1,256]{2,1,0:T(1,128)}, s32[128]{0:T(128)}) custom-call(s32[624]{0:T(1024)} %concatenate.3.ints, f32[3,64,256]{2,1,0:T(8,128)} %pos.1, f32[3,64,256]{2,1,0:T(8,128)} %vel.1, f32[64,256]{1,0:T(8,128)} %energy.1, f32[64,256]{1,0:T(8,128)} %masses.1, ...), custom_call_target="tpu_custom_call" | custom-call | tf_op jit(solution)/shard_map/pallas_call | solution.py:652
  8.3 0.0 copy-start.3
  8.3 0.9 copy-done.3
  9.2 0.0 copy-start.6
  9.3 0.8 copy-done.6
  10.0 0.0 copy-start.7
  10.0 0.7 copy-done.7
  10.7 20.1 %shard_map.113 = (f32[288,8,256]{2,1,0:T(8,128)S(1)}, f32[288,1,256]{2,1,0:T(1,128)S(1)}, s32[9,1,128]{2,1,0:T(1,128)S(1)}, s32[8,128]{1,0:T(8,128)S(1)}) custom-call(f32[32,8,256]{2,1,0:T(8,128)S(1)} %copy-done.3, f32[32,1,256]{2,1,0:T(1,128)S(1)} %copy-done.6, s32[1,1,128]{2,1,0:T(1,128)S(1)} %bitcast.7), custom_call_target="tpu_custom_call" | custom-call | tf_op jit(solution)/shard_map/pallas_call | solution.py:652
  30.8 0.0 copy-start
  30.8 1.0 copy-done
  31.8 0.0 copy-start.4
  31.8 0.7 copy-done.4
  32.5 53.9 %shard_map.114 = (f32[64,1,256]{2,1,0:T(1,128)S(1)}, f32[288,1,256]{2,1,0:T(1,128)S(1)}, s32[1088]{0:T(1024)S(1)}) custom-call(s32[624]{0:T(1024)S(1)} %copy-done.4, s32[9,1,128]{2,1,0:T(1,128)S(1)} %get-tuple-element.25.notes, s32[8,128]{1,0:T(8,128)S(1)} %get-tuple-element.26.shares, f32[64,8,256]{2,1,0:T(8,128)S(1)} %copy-done, ...), custom_call_target="tpu_custom_call" | custom-call | tf_op jit(solution)/shard_map/pallas_call | solution.py:652
  86.4 0.0 copy-start.1
  86.4 0.0 copy-done.2
  86.4 11.2 %shard_map.115 = (f32[64,1,256]{2,1,0:T(1,128)S(1)}, f32[64,2,256]{2,1,0:T(2,128)S(1)}, f32[288,1,256]{2,1,0:T(1,128)S(1)}) custom-call(s32[624]{0:T(1024)S(1)} %copy-done.4, f32[64,8,256]{2,1,0:T(8,128)S(1)} %copy-done, f32[64,8,256]{2,1,0:T(8,128)S(1)} %copy-done.2, f32[64,1,256]{2,1,0:T(1,128)S(1)} %get-tuple-element.28.partial, ...), custom_call_target="tpu_custom_call" | custom-call | tf_op jit(solution)/shard_map/pallas_call | solution.py:652
  97.7 0.0 copy-done.1
  97.7 79.8 %shard_map.116 = (f32[64,4,256]{2,1,0:T(4,128)S(1)}, f32[288,4,256]{2,1,0:T(4,128)S(1)}) custom-call(s32[1088]{0:T(1024)S(1)} %get-tuple-element.31.plan, f32[64,8,256]{2,1,0:T(8,128)S(1)} %copy-done.1, f32[64,8,256]{2,1,0:T(8,128)S(1)} %copy-done.2, f32[64,2,256]{2,1,0:T(2,128)S(1)} %get-tuple-element.32.late, ...), custom_call_target="tpu_custom_call" | custom-call | tf_op jit(solution)/shard_map/pallas_call | solution.py:652
  177.5 0.0 copy-start.5
  177.5 11.8 %shard_map.117.came = f32[288,4,256]{2,1,0:T(4,128)S(1)} custom-call(f32[288,4,256]{2,1,0:T(4,128)S(1)} %get-tuple-element.36.back), custom_call_target="tpu_custom_call" | custom-call | tf_op jit(solution)/shard_map/pallas_call | solution.py:652
  189.3 0.0 copy-done.5
  189.3 1.7 shard_map.118
  (4 shorter events, 0.0 us)
Async XLA Ops:
  8.3 1.0 copy-start.3
  9.2 0.8 copy-start.6
  10.0 0.7 copy-start.7
  30.8 1.0 copy-start
  31.8 0.7 copy-start.4
  32.5 53.9 %copy-start.2 = (f32[64,8,256]{2,1,0:T(8,128)S(1)}, f32[64,8,256]{2,1,0:T(8,128)}, u32[]{:S(2)}) copy-start(f32[64,8,256]{2,1,0:T(8,128)} %get-tuple-element.20.second) | copy-start | bytes 1572868
  86.4 11.3 %copy-start.1 = (f32[64,8,256]{2,1,0:T(8,128)S(1)}, f32[64,8,256]{2,1,0:T(8,128)}, u32[]{:S(2)}) copy-start(f32[64,8,256]{2,1,0:T(8,128)} %get-tuple-element.21.table.first) | copy-start | bytes 1572868
  177.5 11.8 %copy-start.5 = (s32[624]{0:T(1024)S(1)}, s32[624]{0:T(1024)}, u32[]{:S(2)}) copy-start(s32[624]{0:T(1024)} %concatenate.3.ints) | copy-start | bytes 7492

commit v5 on v4

--- a/solution.py
+++ b/solution.py
@@ -320,9 +320,10 @@
     swap_all(sent, late_all, send.at[1], receive.at[1], False)
 
 
-def return_kernel(back, came, send, receive):
+def return_kernel(back, extra, came, send, receive):
     greet(SIDES)
     swap_all(back, came, send, receive, True)
+    extra[...] = total_of(came)
 
 
 def balance(every, shares):
@@ -619,8 +620,7 @@
     over_cells(plan, lay, work)
 
 
-def finish_kernel(ints, second, raw, own, came, density, acceleration, rate, extra, total):
-    extra[...] = total_of(came)
+def finish_kernel(ints, second, raw, own, extra, density, acceleration, rate, total):
     total[...] = own[...]
 
     def add(k, carry):
@@ -744,10 +744,10 @@
     )
     came = call(
         return_kernel,
-        shape(9 * EXPORT, 4, SLOTS),
+        shape(EXPORT, 4, SLOTS),
         [],
         [back],
-        [sems((9,)), sems((9,))],
+        [VMEM((9 * EXPORT, 4, SLOTS), F32), sems((9,)), sems((9,))],
         40,
         2,
     )
@@ -757,7 +757,7 @@
             [shape(CELLS, SLOTS), shape(3, CELLS, SLOTS), shape(CELLS, SLOTS)],
             [ints],
             [second, raw, own, came],
-            [VMEM((EXPORT, 4, SLOTS), F32), VMEM((CELLS, 4, SLOTS), F32)],
+            [VMEM((CELLS, 4, SLOTS), F32)],
         )
     )
 

time: 191 us -> 193 us (1.010)
  the two profiles are of different devices: /device:TPU:67 before, /device:TPU:33 now
where the time goes in v5:
time: 193 us
  Pallas kernels  184 us (95%)
  local copies, waits for them, and re-layouts  6.19 us (3%)
  other arithmetic  2.33 us (1%)
    pallas_call x7, Pallas kernels, call(): pl.pallas_call(kernel, out_shape=out, in_specs=[pl.BlockSpec(memory_space...  184 us
    unnamed x16, local copies, waits for them, and re-layouts  4.09 us

profile of v5, /device:TPU:33, one launch (start us, length us, event | category | flops | bytes accessed | tf_op | source)
XLA Modules:
  0.0 193.0 jit_solution(3860645271203008446)
XLA Ops:
  0.6 0.7 select_reduce_fusion.2
  1.4 0.8 slice_bitcast_fusion
  2.2 0.1 convert_reduce_fusion.3
  2.2 0.2 convert_reduce_fusion.2
  2.4 0.1 select_reduce_fusion.1
  2.5 0.8 multiply_add_fusion
  3.3 0.1 convert_reduce_fusion.1
  3.4 0.2 convert_reduce_fusion
  3.6 0.1 select_reduce_fusion
  3.8 1.3 concatenate.3.ints
  5.1 0.0 copy-start.5
  5.1 3.2 %shard_map.112 = (f32[64,8,256]{2,1,0:T(8,128)}, f32[64,8,256]{2,1,0:T(8,128)}, f32[32,8,256]{2,1,0:T(8,128)}, f32[32,1,256]{2,1,0:T(1,128)}, s32[128]{0:T(128)}) custom-call(s32[624]{0:T(1024)} %concatenate.3.ints, f32[3,64,256]{2,1,0:T(8,128)} %pos.1, f32[3,64,256]{2,1,0:T(8,128)} %vel.1, f32[64,256]{1,0:T(8,128)} %energy.1, f32[64,256]{1,0:T(8,128)} %masses.1, ...), custom_call_target="tpu_custom_call" | custom-call | tf_op jit(solution)/shard_map/pallas_call | solution.py:652
  8.3 0.0 copy-start.3
  8.3 0.9 copy-done.3
  9.3 0.0 copy-start.6
  9.3 0.8 copy-done.6
  10.0 0.0 copy-start.7
  10.0 0.7 copy-done.7
  10.7 21.2 %shard_map.113 = (f32[288,8,256]{2,1,0:T(8,128)S(1)}, f32[288,1,256]{2,1,0:T(1,128)S(1)}, s32[9,1,128]{2,1,0:T(1,128)S(1)}, s32[8,128]{1,0:T(8,128)S(1)}) custom-call(f32[32,8,256]{2,1,0:T(8,128)S(1)} %copy-done.3, f32[32,1,256]{2,1,0:T(1,128)S(1)} %copy-done.6, s32[1,1,128]{2,1,0:T(1,128)S(1)} %bitcast.7), custom_call_target="tpu_custom_call" | custom-call | tf_op jit(solution)/shard_map/pallas_call | solution.py:652
  31.9 0.0 copy-start
  31.9 1.0 copy-done
  32.9 0.0 copy-start.4
  32.9 0.7 copy-done.4
  33.6 0.0 copy-start.2
  33.6 51.2 %shard_map.114 = (f32[64,1,256]{2,1,0:T(1,128)S(1)}, f32[288,1,256]{2,1,0:T(1,128)S(1)}, s32[1088]{0:T(1024)S(1)}) custom-call(s32[624]{0:T(1024)S(1)} %copy-done.4, s32[9,1,128]{2,1,0:T(1,128)S(1)} %get-tuple-element.25.notes, s32[8,128]{1,0:T(8,128)S(1)} %get-tuple-element.26.shares, f32[64,8,256]{2,1,0:T(8,128)S(1)} %copy-done, ...), custom_call_target="tpu_custom_call" | custom-call | tf_op jit(solution)/shard_map/pallas_call | solution.py:652
  84.9 0.0 copy-done.5
  84.9 0.0 copy-done.2
  84.9 13.8 %shard_map.115 = (f32[64,1,256]{2,1,0:T(1,128)S(1)}, f32[64,2,256]{2,1,0:T(2,128)S(1)}, f32[288,1,256]{2,1,0:T(1,128)S(1)}) custom-call(s32[624]{0:T(1024)S(1)} %copy-done.5, f32[64,8,256]{2,1,0:T(8,128)S(1)} %copy-done, f32[64,8,256]{2,1,0:T(8,128)S(1)} %copy-done.2, f32[64,1,256]{2,1,0:T(1,128)S(1)} %get-tuple-element.28.partial, ...), custom_call_target="tpu_custom_call" | custom-call | tf_op jit(solution)/shard_map/pallas_call | solution.py:652
  98.7 0.0 copy-done.1
  98.7 73.5 %shard_map.116 = (f32[64,4,256]{2,1,0:T(4,128)S(1)}, f32[288,4,256]{2,1,0:T(4,128)S(1)}) custom-call(s32[1088]{0:T(1024)S(1)} %get-tuple-element.31.plan, f32[64,8,256]{2,1,0:T(8,128)S(1)} %copy-done.1, f32[64,8,256]{2,1,0:T(8,128)S(1)} %copy-done.2, f32[64,2,256]{2,1,0:T(2,128)S(1)} %get-tuple-element.32.late, ...), custom_call_target="tpu_custom_call" | custom-call | tf_op jit(solution)/shard_map/pallas_call | solution.py:652
  172.2 19.1 %shard_map.117.extra = f32[32,4,256]{2,1,0:T(4,128)S(1)} custom-call(f32[288,4,256]{2,1,0:T(4,128)S(1)} %get-tuple-element.36.back), custom_call_target="tpu_custom_call" | custom-call | tf_op jit(solution)/shard_map/pallas_call | solution.py:652
  191.3 1.6 shard_map.118
  (4 shorter events, 0.0 us)
Async XLA Ops:
  5.1 79.8 %copy-start.5 = (s32[624]{0:T(1024)S(1)}, s32[624]{0:T(1024)}, u32[]{:S(2)}) copy-start(s32[624]{0:T(1024)} %concatenate.3.ints) | copy-start | bytes 7492
  8.3 1.0 copy-start.3
  9.3 0.8 copy-start.6
  10.0 0.7 copy-start.7
  31.9 1.0 copy-start
  32.9 0.7 copy-start.4
  33.6 51.2 %copy-start.2 = (f32[64,8,256]{2,1,0:T(8,128)S(1)}, f32[64,8,256]{2,1,0:T(8,128)}, u32[]{:S(2)}) copy-start(f32[64,8,256]{2,1,0:T(8,128)} %get-tuple-element.20.second) | copy-start | bytes 1572868
  33.6 65.1 %copy-start.1 = (f32[64,8,256]{2,1,0:T(8,128)S(1)}, f32[64,8,256]{2,1,0:T(8,128)}, u32[]{:S(2)}) copy-start(f32[64,8,256]{2,1,0:T(8,128)} %get-tuple-element.21.table.first) | copy-start | bytes 1572868

commit v6 on v5

--- a/solution.py
+++ b/solution.py
@@ -28,7 +28,7 @@
 FORCE_FAR = [(0, 0), (0, 1), (0, 2), (0, 5), (0, 6), (0, 7), (1, 0), (1, 1), (1, 2), (1, 4), (1, 5), (1, 3), (0, 3)]
 
 
-def over_tiles(plan, start, count, block):
+def over_tiles(plan, start, count, block, fours):
     def tile(index):
         entry = plan[start + index]
         return entry // 2, pl.ds(pl.multiple_of((entry % 2) * 128, 128), 128)
@@ -37,16 +37,24 @@
         block((tile(2 * step), tile(2 * step + 1)))
         return carry
 
-    lax.fori_loop(0, count // 2, two, 0)
+    def four(step, carry):
+        block(tuple(tile(4 * step + i) for i in range(4)))
+        return carry
+
+    done = 0
+    if fours:
+        done = count // 4
+        lax.fori_loop(0, done, four, 0)
+    lax.fori_loop(2 * done, count // 2, two, 0)
 
     @pl.when(count % 2 == 1)
     def last():
         block((tile(count - 1),))
 
 
-def over_part(plan, cell, firsts, tiles, block):
+def over_part(plan, cell, firsts, tiles, block, fours=False):
     start = plan[firsts + cell]
-    over_tiles(plan, tiles + start, plan[firsts + cell + 1] - start, block)
+    over_tiles(plan, tiles + start, plan[firsts + cell + 1] - start, block, fours)
 
 
 def flipped(row):
@@ -465,6 +473,7 @@
         over_part(
             plan, cell, LOCAL_FIRST, LOCAL_TILES,
             lambda lanes: density_lanes(held, base, count, table, lanes, raw, False, None),
+            True,
         )
 
         @pl.when(slot >= 0)
@@ -473,6 +482,7 @@
             over_part(
                 plan, cell, CROSS_FIRST, CROSS_TILES,
                 lambda lanes: density_lanes(held, base, count, imports, lanes, back, True, sums),
+                True,
             )
 
             def finish(l):

time: 193 us -> 191 us (0.990)
  the two profiles are of different devices: /device:TPU:33 before, /device:TPU:1 now
where the time goes in v6:
time: 191 us; the launch traced here: 188 us
  Pallas kernels  179 us (94%)
  local copies, waits for them, and re-layouts  6.19 us (3%)
  other arithmetic  2.33 us (1%)
    pallas_call x7, Pallas kernels, call(): pl.pallas_call(kernel, out_shape=out, in_specs=[pl.BlockSpec(memory_space...  179 us
    unnamed x16, local copies, waits for them, and re-layouts  4.09 us

profile of v6, /device:TPU:1, one launch (start us, length us, event | category | flops | bytes accessed | tf_op | source)
XLA Modules:
  0.0 188.2 jit_solution(511026012838809938)
XLA Ops:
  0.6 0.7 select_reduce_fusion.2
  1.4 0.8 slice_bitcast_fusion
  2.2 0.1 convert_reduce_fusion.3
  2.2 0.2 convert_reduce_fusion.2
  2.4 0.1 select_reduce_fusion.1
  2.5 0.8 multiply_add_fusion
  3.3 0.1 convert_reduce_fusion.1
  3.4 0.2 convert_reduce_fusion
  3.6 0.1 select_reduce_fusion
  3.8 1.3 concatenate.3.ints
  5.1 0.0 copy-start.5
  5.1 3.2 %shard_map.112 = (f32[64,8,256]{2,1,0:T(8,128)}, f32[64,8,256]{2,1,0:T(8,128)}, f32[32,8,256]{2,1,0:T(8,128)}, f32[32,1,256]{2,1,0:T(1,128)}, s32[128]{0:T(128)}) custom-call(s32[624]{0:T(1024)} %concatenate.3.ints, f32[3,64,256]{2,1,0:T(8,128)} %pos.1, f32[3,64,256]{2,1,0:T(8,128)} %vel.1, f32[64,256]{1,0:T(8,128)} %energy.1, f32[64,256]{1,0:T(8,128)} %masses.1, ...), custom_call_target="tpu_custom_call" | custom-call | tf_op jit(solution)/shard_map/pallas_call | solution.py:662
  8.3 0.0 copy-start.3
  8.3 0.9 copy-done.3
  9.3 0.0 copy-start.6
  9.3 0.8 copy-done.6
  10.0 0.0 copy-start.7
  10.0 0.7 copy-done.7
  10.7 23.5 %shard_map.113 = (f32[288,8,256]{2,1,0:T(8,128)S(1)}, f32[288,1,256]{2,1,0:T(1,128)S(1)}, s32[9,1,128]{2,1,0:T(1,128)S(1)}, s32[8,128]{1,0:T(8,128)S(1)}) custom-call(f32[32,8,256]{2,1,0:T(8,128)S(1)} %copy-done.3, f32[32,1,256]{2,1,0:T(1,128)S(1)} %copy-done.6, s32[1,1,128]{2,1,0:T(1,128)S(1)} %bitcast.7), custom_call_target="tpu_custom_call" | custom-call | tf_op jit(solution)/shard_map/pallas_call | solution.py:662
  34.2 0.0 copy-start
  34.2 1.0 copy-done
  35.2 0.0 copy-start.4
  35.2 0.7 copy-done.4
  35.9 0.0 copy-start.2
  35.9 41.2 %shard_map.114 = (f32[64,1,256]{2,1,0:T(1,128)S(1)}, f32[288,1,256]{2,1,0:T(1,128)S(1)}, s32[1088]{0:T(1024)S(1)}) custom-call(s32[624]{0:T(1024)S(1)} %copy-done.4, s32[9,1,128]{2,1,0:T(1,128)S(1)} %get-tuple-element.25.notes, s32[8,128]{1,0:T(8,128)S(1)} %get-tuple-element.26.shares, f32[64,8,256]{2,1,0:T(8,128)S(1)} %copy-done, ...), custom_call_target="tpu_custom_call" | custom-call | tf_op jit(solution)/shard_map/pallas_call | solution.py:662
  77.1 0.0 copy-done.5
  77.1 0.0 copy-done.2
  77.1 20.5 %shard_map.115 = (f32[64,1,256]{2,1,0:T(1,128)S(1)}, f32[64,2,256]{2,1,0:T(2,128)S(1)}, f32[288,1,256]{2,1,0:T(1,128)S(1)}) custom-call(s32[624]{0:T(1024)S(1)} %copy-done.5, f32[64,8,256]{2,1,0:T(8,128)S(1)} %copy-done, f32[64,8,256]{2,1,0:T(8,128)S(1)} %copy-done.2, f32[64,1,256]{2,1,0:T(1,128)S(1)} %get-tuple-element.28.partial, ...), custom_call_target="tpu_custom_call" | custom-call | tf_op jit(solution)/shard_map/pallas_call | solution.py:662
  97.6 0.0 copy-done.1
  97.6 55.4 %shard_map.116 = (f32[64,4,256]{2,1,0:T(4,128)S(1)}, f32[288,4,256]{2,1,0:T(4,128)S(1)}) custom-call(s32[1088]{0:T(1024)S(1)} %get-tuple-element.31.plan, f32[64,8,256]{2,1,0:T(8,128)S(1)} %copy-done.1, f32[64,8,256]{2,1,0:T(8,128)S(1)} %copy-done.2, f32[64,2,256]{2,1,0:T(2,128)S(1)} %get-tuple-element.32.late, ...), custom_call_target="tpu_custom_call" | custom-call | tf_op jit(solution)/shard_map/pallas_call | solution.py:662
  153.0 33.6 %shard_map.117.extra = f32[32,4,256]{2,1,0:T(4,128)S(1)} custom-call(f32[288,4,256]{2,1,0:T(4,128)S(1)} %get-tuple-element.36.back), custom_call_target="tpu_custom_call" | custom-call | tf_op jit(solution)/shard_map/pallas_call | solution.py:662
  186.6 1.6 shard_map.118
  (4 shorter events, 0.0 us)
Async XLA Ops:
  5.1 72.0 %copy-start.5 = (s32[624]{0:T(1024)S(1)}, s32[624]{0:T(1024)}, u32[]{:S(2)}) copy-start(s32[624]{0:T(1024)} %concatenate.3.ints) | copy-start | bytes 7492
  8.3 1.0 copy-start.3
  9.3 0.8 copy-start.6
  10.0 0.7 copy-start.7
  34.2 1.0 copy-start
  35.2 0.7 copy-start.4
  35.9 41.2 %copy-start.2 = (f32[64,8,256]{2,1,0:T(8,128)S(1)}, f32[64,8,256]{2,1,0:T(8,128)}, u32[]{:S(2)}) copy-start(f32[64,8,256]{2,1,0:T(8,128)} %get-tuple-element.20.second) | copy-start | bytes 1572868
  35.9 61.7 %copy-start.1 = (f32[64,8,256]{2,1,0:T(8,128)S(1)}, f32[64,8,256]{2,1,0:T(8,128)}, u32[]{:S(2)}) copy-start(f32[64,8,256]{2,1,0:T(8,128)} %get-tuple-element.21.table.first) | copy-start | bytes 1572868
